TPU v7x, 128 devices: a whole 4x4x4 slice. The times are simulated.
128 devices in a mesh: rows: 32 (over z, y, core), cols: 4 (over x).
Axes of the slice: x: 4, y: 4, z: 4, core: 2. Of those that a mesh axis runs over, the one named last changes fastest.
Arguments:
- activations: bfloat16 [8192, 65536], P('rows', 'cols'), as said below
- weight_tiles: bfloat16 [4, 64, 8, 128, 128], P('cols', 'rows'), may hold values from -0.1875 to 0.1875
- panel_map: int32 [4, 64], P('cols'), may hold values from 0 to 63, each once within a row
- block_index: int32 [256, 8], replicated, may hold values from 0 to 511, all different within a row
- active_list: int32 [32, 16], P('rows'), may hold values from 0 to 16, as said below
- bias: float32 [32768], P('cols'), may hold values from -1 to 0.5
Outputs:
- output: bfloat16 [8192, 32768], P('rows', 'cols')
Inputs may be any that keep to these rules, and one draw needn't show every extreme that they name: Each row of panel_map holds every number of its range once. `block_index`: each output block column names 8 different input blocks; every input block is named by some column. `active_list`: each row group lists 16 // 2 to 16 different active row blocks below 16 in its first slots, in no particular order; its remaining slots hold 16. At least one row group has 16 active row blocks. `activations`: entries are zero or positive; row scales differ widely from sample to sample.
All inputs are finite; a program needn't handle non-finite values.
Results may differ from a plain program's by a relative error of at most 0.001.
Values may be sent and summed in bfloat16 or wider, within the bound.
A program may use at most 256 MiB of HBM per device.

v0:
```python
import jax
import jax.numpy as jnp
from jax import lax
from jax.sharding import PartitionSpec as P

TILE = 128
ROW_BLOCK = 16


def body(activations, weight_tiles, panel_map, block_index, active_list, bias):
    row_count, local_width = activations.shape
    blocks_here = row_count // ROW_BLOCK
    listed = active_list[0]
    picked = jnp.minimum(listed, blocks_here - 1)
    gathered = lax.all_gather(activations, "cols", axis=1, tiled=True)
    compact = jnp.take(gathered.reshape(blocks_here, ROW_BLOCK, -1), picked, axis=0)
    slot_rows = compact.shape[0] * ROW_BLOCK
    tile_view = compact.reshape(slot_rows, -1, TILE)
    panels_here = panel_map.shape[1]
    columns = lax.axis_index("cols") * panels_here + panel_map[0]
    sources = jnp.take(block_index, columns, axis=0)
    panel_block = lax.all_gather(weight_tiles[0], "rows", axis=0, tiled=True)
    count_here = panel_block.shape[0]
    total = jnp.zeros((slot_rows, count_here, TILE), jnp.float32)
    for depth in range(panel_block.shape[1]):
        chosen = jnp.take(tile_view, sources[:, depth], axis=1)
        total = total + jnp.einsum(
            "mpt,pts->mps", chosen, panel_block[:, depth], preferred_element_type=jnp.float32
        )
    ordered = jnp.take(total, jnp.argsort(panel_map[0]), axis=1).reshape(slot_rows, -1)
    clamped = jnp.minimum(jnp.maximum(ordered + bias[None, :], 0.0), 32.0).astype(jnp.bfloat16)
    placing = (listed[:, None] == jnp.arange(blocks_here, dtype=jnp.int32)[None, :]).astype(
        jnp.bfloat16
    )
    spread = jnp.einsum(
        "sb,srw->brw",
        placing,
        clamped.reshape(listed.shape[0], ROW_BLOCK, -1),
        preferred_element_type=jnp.float32,
    )
    return spread.astype(jnp.bfloat16).reshape(row_count, -1)


def solution(mesh):
    in_specs = (
        P("rows", "cols"),
        P("cols", "rows", None, None, None),
        P("cols", None),
        P(),
        P("rows", None),
        P("cols"),
    )
    out_specs = P("rows", "cols")
    return jax.shard_map(body, mesh=mesh, in_specs=in_specs, out_specs=out_specs, check_vma=False)
```

profile of v0, /device:TPU:0, one launch (start us, length us, event | category | flops | bytes accessed | tf_op | source)
XLA Modules:
  0.0 584.6 jit_solution(9170330887527009049)
XLA Ops:
  6.5 0.0 all-gather.4.cloned.1.call-start
  6.6 0.7 all-gather.4.cloned.1.call-update
  7.3 0.0 all-gather.6.cloned.1.call-start
  7.3 0.3 copy-done.7
  7.6 0.8 copy.16
  8.4 0.0 all-gather.6.cloned.1.call-update
  8.4 0.0 copy-done.11
  8.5 0.1 broadcast_in_dim.54
  8.5 0.1 broadcast_in_dim.55
  8.6 0.0 copy-done.10
  8.6 0.1 copy.14
  8.8 2.0 sort.17
  10.8 0.6 gather_fusion
  11.5 0.6 pad_clamp_fusion
  12.1 0.1 broadcast_select_fusion
  12.2 0.3 slice_reduce_fusion.7
  12.7 0.7 broadcast_bitcast_fusion
  13.4 292.0 %all-gather.4.cloned.1.call-done = bf16[256,65536]{1,0:T(8,128)(2,1)} async-done(((bf16[256,16384]{1,0:T(8,128)(2,1)}), bf16[256,65536]{1,0:T(8,128)(2,1)}) %all-gather.4.cloned.1.call-update) | async-done | bytes 33554448 | tf_op jit(solution)/shard_map/all_gather | solution.py:15
  305.4 22.6 %fusion.56 = (bf16[16,16,32768]{2,1,0:T(8,128)(2,1)}, bf16[16,16,32768]{2,1,0:T(8,128)(2,1)}) fusion(bf16[16,16,65536]{2,1,0:T(8,128)(2,1)} %bitcast.79), kind=kLoop, calls=%fused_computation.124 | loop fusion | bytes 67108864 | tf_op jit(solution)/shard_map/jit(_take)/gather | solution.py:16
  328.0 13.3 %gather_fusion.3 = bf16[16,16,32768]{2,1,0:T(8,128)(2,1)} fusion(bf16[16,16,32768]{2,1,0:T(8,128)(2,1)} %get-tuple-element.17, s32[1024]{0:T(1024)S(1)} %pad_clamp_fusion.9), kind=kCustom, calls=%fused_computation.11 | custom fusion | bytes 33554496 | tf_op jit(solution)/shard_map/jit(_take)/gather | solution.py:16
  341.2 14.5 %gather_fusion.2 = bf16[16,16,32768]{2,1,0:T(8,128)(2,1)} fusion(bf16[16,16,32768]{2,1,0:T(8,128)(2,1)} %get-tuple-element.16, s32[1024]{0:T(1024)S(1)} %pad_clamp_fusion.9), kind=kCustom, calls=%fused_computation.10 | custom fusion | bytes 33554496 | tf_op jit(solution)/shard_map/jit(_take)/gather | solution.py:16
  355.8 24.0 %pad_maximum_fusion = bf16[16,16,65536]{2,1,0:T(8,128)(2,1)} fusion(bf16[16,16,32768]{2,1,0:T(8,128)(2,1)} %gather_fusion.3, bf16[16,16,32768]{2,1,0:T(8,128)(2,1)} %gather_fusion.2), kind=kLoop, calls=%fused_computation.12 | loop fusion | flops 67108864 | bytes 67108864
  379.8 23.1 %copy.20 = bf16[32,8,512,128]{3,2,1,0:T(8,128)(2,1)} copy(bf16[32,8,512,128]{3,1,2,0:T(8,128)(2,1)} %bitcast.77) | data formatting | bytes 67108864
  402.9 29.7 %copy_select_fusion = bf16[256,512,128]{2,0,1:T(8,128)(2,1)} fusion(bf16[256,512,128]{2,1,0:T(8,128)(2,1)} %bitcast.76, pred[256]{0:T(512)(128)(4,1)S(1)} %broadcast_in_dim.55), kind=kLoop, calls=%fused_computation.13 | loop fusion | flops 16777216 | bytes 67109120 | tf_op jit(solution)/shard_map/jit(_take)/select_n | solution.py:16
  432.6 4.9 gather_fusion.4
  437.5 4.9 gather_fusion.10
  442.4 5.0 gather_fusion.8
  447.5 4.9 gather_fusion.6
  452.4 4.9 gather_fusion.5
  457.3 5.0 gather_fusion.11
  462.3 4.9 gather_fusion.9
  467.3 5.0 gather_fusion.7
  472.3 8.6 %fusion.8 = f32[64,256,128]{2,1,0:T(8,128)} fusion(bf16[64,256,128]{2,1,0:T(8,128)(2,1)} %gather_fusion.7, pred[64]{0:T(512)(128)(4,1)S(1)} %get-tuple-element.30, bf16[64,8,128,128]{3,2,0,1:T(8,128)(2,1)} %bitcast.80), kind=kOutput, calls=%fused_computation.25 | convolution fusion | flops 538968064 | bytes 14680128 | tf_op jit(solution)/shard_map/mpt,pts->mps/dot_general | solution.py:27
  480.9 7.0 %fusion.4 = f32[64,256,128]{2,1,0:T(8,128)} fusion(bf16[64,256,128]{2,1,0:T(8,128)(2,1)S(1)} %copy-done.5, pred[64]{0:T(512)(128)(4,1)S(1)} %get-tuple-element.28, bf16[64,8,128,128]{3,2,0,1:T(8,128)(2,1)} %bitcast.81), kind=kOutput, calls=%fused_computation.21 | convolution fusion | flops 538968064 | bytes 14680128 | tf_op jit(solution)/shard_map/mpt,pts->mps/dot_general | solution.py:27
  487.9 0.0 copy-done.6
  487.9 4.5 fusion
  492.4 0.0 copy-done.3
  492.4 4.5 fusion.12
  497.0 4.5 fusion.10
  501.5 4.5 fusion.6
  506.0 4.7 fusion.2
  510.7 24.9 %add_bitcast_fusion = f32[256,64,128]{2,0,1:T(8,128)} fusion(f32[64,256,128]{2,1,0:T(8,128)} %fusion, f32[64,256,128]{2,1,0:T(8,128)} %fusion.2, f32[64,256,128]{2,1,0:T(8,128)} %fusion.4, f32[64,256,128]{2,1,0:T(8,128)} %fusion.6, f32[64,256,128]{2,1,0:T(8,128)} %fusion.8, f32[64,256,128]{2,1,0:T(8,128)} %fusion.10, f32[64,256,128]{2,1,0:T(8,128)} %fusion.12, ...), kind=kOutput, calls=%fused_computation.15 | convolution fusion | flops 553648128 | bytes 73400384 | tf_op jit(solution)/shard_map/mpt,pts->mps/dot_general | solution.py:27
  535.6 7.8 %gather_fusion.1 = f32[64,256,128]{2,1,0:T(8,128)} fusion(f32[256,64,128]{2,0,1:T(8,128)} %add_bitcast_fusion, s32[1024]{0:T(1024)} %pad_clamp_fusion), kind=kCustom, calls=%fused_computation.9 | custom fusion | bytes 16777472 | tf_op jit(solution)/shard_map/jit(_take)/gather | solution.py:30
  543.4 11.4 %copy.17 = f32[256,64,128]{2,1,0:T(8,128)} copy(f32[256,64,128]{2,0,1:T(8,128)} %bitcast.78) | data formatting | bytes 16777216 | tf_op jit(solution)/shard_map/jit(_take)/gather | solution.py:30
  554.9 9.4 %gather.23 = f32[16,16,8192]{2,1,0:T(8,128)} reshape(f32[256,64,128]{2,1,0:T(8,128)} %copy.17) | data formatting | bytes 16777216 | tf_op jit(solution)/shard_map/jit(_take)/gather | solution.py:30
  564.3 4.5 clamp_convert_fusion
  568.8 4.7 convolution_convert_fusion
  573.5 4.3 copy.19
  (49 shorter events, 0.2 us)
Async XLA Ops:
  6.5 1.0 copy-start.7
  6.5 1.9 copy-start.11
  6.5 2.1 copy-start.10
  6.5 2.2 copy-start.13
  6.5 298.9 %all-gather.4.cloned.1.call-start = ((), (), s32[]{:S(2)}) async-start(), calls=%async_computation | async-start | bytes 41943040 | tf_op jit(solution)/shard_map/all_gather | solution.py:15
  7.3 465.0 %all-gather.6.cloned.1.call-start = ((), (), s32[]{:S(2)}) async-start(), calls=%async_computation.1 | async-start | bytes 17301504 | tf_op jit(solution)/shard_map/all_gather | solution.py:22
  472.3 8.6 %copy-start.5 = (bf16[64,256,128]{2,1,0:T(8,128)(2,1)S(1)}, bf16[64,256,128]{2,1,0:T(8,128)(2,1)}, u32[]{:S(2)}) copy-start(bf16[64,256,128]{2,1,0:T(8,128)(2,1)} %gather_fusion.9) | copy-start | bytes 12582916
  472.3 15.6 %copy-start.6 = (bf16[1,64,8,128,128]{4,3,1,2,0:T(8,128)(2,1)S(1)}, bf16[1,64,8,128,128]{4,3,1,2,0:T(8,128)(2,1)}, u32[]{:S(2)}) copy-start(bf16[1,64,8,128,128]{4,3,1,2,0:T(8,128)(2,1)} %all-gather.6.cloned.1.call-done) | copy-start | bytes 50331652
  480.9 7.1 %copy-start.4 = (bf16[64,256,128]{2,1,0:T(8,128)(2,1)S(1)}, bf16[64,256,128]{2,1,0:T(8,128)(2,1)}, u32[]{:S(2)}) copy-start(bf16[64,256,128]{2,1,0:T(8,128)(2,1)} %gather_fusion.11) | copy-start | bytes 12582916
  487.9 4.5 copy-start.3
  492.4 4.5 copy-start.2
  497.0 4.5 copy-start.1
  501.5 4.5 copy-start
  554.9 9.4 %copy-start.8 = (f32[8192]{0:T(1024)S(1)}, f32[8192]{0:T(1024)}, u32[]{:S(2)}) copy-start(f32[8192]{0:T(1024)} %param.13) | copy-start | bytes 98308
  554.9 9.4 %copy-start.9 = (pred[8192]{0:T(1024)(128)(4,1)S(1)}, pred[8192]{0:T(1024)(128)(4,1)}, u32[]{:S(2)}) copy-start(pred[8192]{0:T(1024)(128)(4,1)} %broadcast_bitcast_fusion) | copy-start | bytes 24580
  564.3 4.5 copy-start.12
Sparse Core Ops, SparseCore 0:
  9.0 296.2 all-gather.3
  307.7 73.6 all-gather.5
where the time goes:
time: 586 us; the launch traced here: 585 us
  waiting for transfers between devices  293 us (50%)
  local copies, waits for them, and re-layouts  149 us (25%)
  matrix products  68 us (12%)
  other arithmetic  61 us (10%)
  between operations  13.6 us (2%)
    all_gather x1, waiting for transfers between devices, body(): gathered = lax.all_gather(activations, 'cols', axis=1, tiled=True)  292 us
    dot_general x8, matrix products, body(): jnp.einsum('mpt,pts->mps', chosen, panel_block[:, depth], preferred_eleme...  63.3 us
    gather x3, local copies, waits for them, and re-layouts, body(): jnp.take(gathered.reshape(blocks_here, ROW_BLOCK, -1), picked, axis=0)  50.4 us
    gather x8, local copies, waits for them, and re-layouts, body(): chosen = jnp.take(tile_view, sources[:, depth], axis=1)  39.8 us
    select_n x2, other arithmetic, body(): jnp.take(gathered.reshape(blocks_here, ROW_BLOCK, -1), picked, axis=0)  29.7 us
    gather x3, local copies, waits for them, and re-layouts, body(): jnp.take(total, jnp.argsort(panel_map[0]), axis=1).reshape(slot_rows, -1)  28.6 us
    unnamed x31, local copies, waits for them, and re-layouts  24.4 us
    unnamed x1, other arithmetic  24 us
  transfers between devices with their start and end apart: 2, of which 1 were waited for; matrix products, arithmetic and copies ran while one was open for 30% of the time, Pallas kernels for 0%

commit v1 on v0

--- a/solution.py
+++ b/solution.py
@@ -1,13 +1,255 @@
+import functools
+
 import jax
 import jax.numpy as jnp
 from jax import lax
+from jax.experimental import pallas as pl
+from jax.experimental.pallas import tpu as pltpu
 from jax.sharding import PartitionSpec as P
 
 TILE = 128
 ROW_BLOCK = 16
-
-
-def body(activations, weight_tiles, panel_map, block_index, active_list, bias):
+GROUPS = 4
+PANELS = 64
+DEPTH = 8
+HERE = 128
+LISTED = 98
+PASSED = 48
+OWN, LEFT = 0, HERE
+RIGHT = LEFT + LISTED
+FAR_LEFT = RIGHT + LISTED
+FAR_RIGHT = FAR_LEFT + PASSED
+SLOTS = FAR_RIGHT + PASSED
+MESH = pl.DeviceIdType.MESH
+
+
+def plan_kernel(place_ref, index_ref, map_ref, lists_ref, table_ref):
+    place = place_ref[0]
+    blocks = GROUPS * HERE
+    lane = lax.broadcasted_iota(jnp.int32, (GROUPS * PANELS, blocks), 1)
+    named = jnp.zeros((GROUPS * PANELS, blocks), jnp.float32)
+    for k in range(DEPTH):
+        named = jnp.where(index_ref[:, k : k + 1] == lane, 1.0, named)
+    need = [jnp.max(named[c * PANELS : (c + 1) * PANELS], axis=0, keepdims=True) for c in range(GROUPS)]
+
+    def asked(distance):
+        return jnp.concatenate(
+            [need[(s + distance) % GROUPS][:, s * HERE : (s + 1) * HERE] for s in range(GROUPS)], axis=0
+        )
+
+    right, far, left = asked(1), asked(2), asked(3)
+    row = lax.broadcasted_iota(jnp.int32, (HERE, HERE), 0)
+    col = lax.broadcasted_iota(jnp.int32, (HERE, HERE), 1)
+    before = (row < col).astype(jnp.bfloat16)
+
+    def rank(flags):
+        return jnp.dot(flags.astype(jnp.bfloat16), before, preferred_element_type=jnp.float32)
+
+    def count(flags):
+        return jnp.sum(flags, axis=1, keepdims=True)
+
+    both = far * right * left
+    none = far * (1.0 - right) * (1.0 - left)
+    only_right = far * right * (1.0 - left)
+    only_left = far * left * (1.0 - right)
+    none_n, both_n = count(none), count(both)
+    cut = jnp.clip(jnp.floor((count(left) - count(right) + none_n) * 0.5), 0.0, none_n)
+    tilt = count(only_left) + none_n - cut - count(only_right) - cut
+    share = jnp.clip(jnp.floor((tilt + both_n) * 0.5), 0.0, both_n)
+    by_right = only_right + none * (rank(none) < cut) + both * (rank(both) < share)
+    by_left = far - by_right
+
+    def order(passed, wanted):
+        rest = wanted * (1.0 - passed)
+        at = jnp.where(passed > 0.0, rank(passed), count(passed) + rank(rest))
+        inside = passed + rest
+        return jnp.where(inside > 0.0, at, -1.0), count(passed), count(inside)
+
+    at_right, passed_right, listed_right = order(by_right, right)
+    at_left, passed_left, listed_left = order(by_left, left)
+    passed_most = jnp.max(jnp.maximum(passed_right, passed_left), axis=0, keepdims=True)
+    listed_most = jnp.max(jnp.maximum(listed_right, listed_left), axis=0, keepdims=True)
+
+    source = lax.broadcasted_iota(jnp.int32, (GROUPS, HERE), 0)
+    mine = source == place
+    slot = lax.broadcasted_iota(jnp.int32, (HERE, HERE), 0).astype(jnp.float32)
+    ids = lax.broadcasted_iota(jnp.int32, (8, HERE), 1).astype(jnp.bfloat16)
+
+    def listing(at):
+        own = jnp.sum(jnp.where(mine, at, 0.0), axis=0, keepdims=True)
+        hot = (own == slot).astype(jnp.bfloat16)
+        out = lax.dot_general(ids, hot, (((1,), (1,)), ((), ())), preferred_element_type=jnp.float32)
+        return out[:1]
+
+    lists_ref[...] = jnp.concatenate(
+        [
+            listing(at_right),
+            listing(at_left),
+            jnp.broadcast_to(passed_most, (1, HERE)),
+            jnp.broadcast_to(listed_most, (1, HERE)),
+            jnp.zeros((4, HERE), jnp.float32),
+        ],
+        axis=0,
+    ).astype(jnp.int32)
+
+    ids_here = lax.broadcasted_iota(jnp.int32, (GROUPS, HERE), 1).astype(jnp.float32)
+    from_left = LEFT + at_right
+    from_right = RIGHT + at_left
+    from_far = jnp.where(by_right > 0.0, FAR_LEFT + at_right, FAR_RIGHT + at_left)
+    away = lax.rem(source - place + GROUPS, GROUPS)
+    slots = jnp.where(
+        away == 0,
+        OWN + ids_here,
+        jnp.where(away == 1, from_right, jnp.where(away == 2, from_far, from_left)),
+    )
+    slots = jnp.concatenate([slots[s : s + 1] for s in range(GROUPS)], axis=1)
+    mine_index = index_ref[pl.ds(pl.multiple_of(place * PANELS, PANELS), PANELS), :]
+    lane = lax.broadcasted_iota(jnp.int32, (PANELS, blocks), 1)
+    columns = []
+    for k in range(DEPTH):
+        hit = mine_index[:, k : k + 1] == lane
+        columns.append(jnp.sum(jnp.where(hit, slots, 0.0), axis=1, keepdims=True))
+    panel = lax.broadcasted_iota(jnp.int32, (PANELS, PANELS), 0)
+    stored = lax.broadcasted_iota(jnp.int32, (PANELS, PANELS), 1).astype(jnp.float32)
+    columns.append(jnp.sum(jnp.where(map_ref[...] == panel, stored, 0.0), axis=1, keepdims=True))
+    columns.append(jnp.zeros((PANELS, 7), jnp.float32))
+    table_ref[...] = jnp.concatenate(columns, axis=1).astype(jnp.int32)
+
+
+def plan(place, block_index, panel_map):
+    return pl.pallas_call(
+        plan_kernel,
+        out_shape=(
+            jax.ShapeDtypeStruct((8, HERE), jnp.int32),
+            jax.ShapeDtypeStruct((PANELS, 16), jnp.int32),
+        ),
+        in_specs=[
+            pl.BlockSpec(memory_space=pltpu.SMEM),
+            pl.BlockSpec(memory_space=pltpu.VMEM),
+            pl.BlockSpec(memory_space=pltpu.VMEM),
+        ],
+        out_specs=(pl.BlockSpec(memory_space=pltpu.VMEM), pl.BlockSpec(memory_space=pltpu.VMEM)),
+        compiler_params=pltpu.CompilerParams(vmem_limit_bytes=16 << 20),
+        name="plan",
+    )(place, block_index, panel_map)
+
+
+def exchange_kernel(lists_ref, act_ref, pool_ref, act, to_right, to_left, send, recv, load, own):
+    me = lax.axis_index("cols")
+    right, left = lax.rem(me + 1, GROUPS), lax.rem(me + GROUPS - 1, GROUPS)
+    reads = []
+    for s in range(HERE):
+        reads.append(pltpu.make_async_copy(act_ref.at[:, pl.ds(s * TILE, TILE)], act.at[s], load.at[s]))
+        reads[-1].start()
+    barrier = pltpu.get_barrier_semaphore()
+    for neighbour in (left, right):
+        pl.semaphore_signal(barrier, inc=1, device_id={"cols": neighbour}, device_id_type=MESH)
+    for read in reads:
+        read.wait()
+
+    def pack(row, buffer, start, stop):
+        def one(s, carry):
+            buffer[s] = act[lists_ref[row, s]]
+            return carry
+
+        lax.fori_loop(start, stop, one, 0)
+
+    def ship(n, src, dst, to):
+        copy = pltpu.make_async_remote_copy(
+            src_ref=src,
+            dst_ref=pool_ref.at[pl.ds(dst, src.shape[0])],
+            send_sem=send.at[n],
+            recv_sem=recv.at[n],
+            device_id={"cols": to},
+            device_id_type=MESH,
+        )
+        copy.start()
+        return copy
+
+    pack(0, to_right, 0, PASSED)
+    pack(1, to_left, 0, PASSED)
+    pl.semaphore_wait(barrier, 2)
+    rest = LISTED - PASSED
+    head_right = ship(0, to_right.at[pl.ds(0, PASSED)], LEFT, right)
+    head_left = ship(1, to_left.at[pl.ds(0, PASSED)], RIGHT, left)
+    pack(0, to_right, PASSED, LISTED)
+    pack(1, to_left, PASSED, LISTED)
+    tail_right = ship(2, to_right.at[pl.ds(PASSED, rest)], LEFT + PASSED, right)
+    tail_left = ship(3, to_left.at[pl.ds(PASSED, rest)], RIGHT + PASSED, left)
+    keep = pltpu.make_async_copy(act, pool_ref.at[pl.ds(OWN, HERE)], own)
+    keep.start()
+    head_right.wait_recv()
+    on_right = ship(4, pool_ref.at[pl.ds(LEFT, PASSED)], FAR_LEFT, right)
+    head_left.wait_recv()
+    on_left = ship(5, pool_ref.at[pl.ds(RIGHT, PASSED)], FAR_RIGHT, left)
+    head_right.wait_send()
+    head_left.wait_send()
+    keep.wait()
+    for copy in (tail_right, tail_left, on_right, on_left):
+        copy.wait()
+
+
+def exchange(lists, activations):
+    rows = activations.shape[0]
+    return pl.pallas_call(
+        exchange_kernel,
+        out_shape=jax.ShapeDtypeStruct((SLOTS, rows, TILE), jnp.bfloat16),
+        in_specs=[pl.BlockSpec(memory_space=pltpu.SMEM), pl.BlockSpec(memory_space=pl.ANY)],
+        out_specs=pl.BlockSpec(memory_space=pl.ANY),
+        scratch_shapes=[
+            pltpu.VMEM((HERE, rows, TILE), jnp.bfloat16),
+            pltpu.VMEM((LISTED, rows, TILE), jnp.bfloat16),
+            pltpu.VMEM((LISTED, rows, TILE), jnp.bfloat16),
+            pltpu.SemaphoreType.DMA((6,)),
+            pltpu.SemaphoreType.DMA((6,)),
+            pltpu.SemaphoreType.DMA((HERE,)),
+            pltpu.SemaphoreType.DMA,
+        ],
+        compiler_params=pltpu.CompilerParams(
+            collective_id=0, has_side_effects=True, vmem_limit_bytes=40 << 20
+        ),
+        cost_estimate=pl.CostEstimate(flops=0, bytes_accessed=600 << 20, transcendentals=0),
+        name="exchange",
+    )(lists, activations)
+
+
+def sums_kernel(table_ref, *refs):
+    taken, (weight_ref, bias_ref, live_ref, out_ref) = refs[:DEPTH], refs[DEPTH:]
+    j = pl.program_id(0)
+    inputs = jnp.concatenate([ref[0] for ref in taken], axis=1)
+    weights = weight_ref[0].reshape(DEPTH * TILE, TILE)
+    total = jnp.dot(inputs, weights, preferred_element_type=jnp.float32)
+    total = jnp.clip(total + bias_ref[pl.ds(j, 1), :], 0.0, 32.0)
+    out_ref[...] = jnp.where(live_ref[...] > 0.0, total, 0.0).astype(jnp.bfloat16)
+
+
+def sums(table, pool, panels, bias, live):
+    rows = pool.shape[1]
+    taken = [
+        pl.BlockSpec((1, rows, TILE), functools.partial(lambda k, j, t: (t[j, k], 0, 0), k))
+        for k in range(DEPTH)
+    ]
+    return pl.pallas_call(
+        sums_kernel,
+        out_shape=jax.ShapeDtypeStruct((rows, PANELS * TILE), jnp.bfloat16),
+        grid_spec=pltpu.PrefetchScalarGridSpec(
+            num_scalar_prefetch=1,
+            grid=(PANELS,),
+            in_specs=taken
+            + [
+                pl.BlockSpec((1, DEPTH, TILE, TILE), lambda j, t: (t[j, DEPTH], 0, 0, 0)),
+                pl.BlockSpec((PANELS, TILE), lambda j, t: (0, 0)),
+                pl.BlockSpec((rows, 1), lambda j, t: (0, 0)),
+            ],
+            out_specs=pl.BlockSpec((rows, TILE), lambda j, t: (0, j)),
+        ),
+        compiler_params=pltpu.CompilerParams(vmem_limit_bytes=32 << 20),
+        cost_estimate=pl.CostEstimate(flops=4 << 30, bytes_accessed=52 << 20, transcendentals=0),
+        name="sums",
+    )(table, *([pool] * DEPTH), panels, bias, live)
+
+
+def general(activations, weight_tiles, panel_map, block_index, active_list, bias):
     row_count, local_width = activations.shape
     blocks_here = row_count // ROW_BLOCK
     listed = active_list[0]
@@ -41,6 +283,27 @@
     return spread.astype(jnp.bfloat16).reshape(row_count, -1)
 
 
+def body(activations, weight_tiles, panel_map, block_index, active_list, bias):
+    place = lax.axis_index("cols").astype(jnp.int32).reshape(1)
+    lists, table = plan(place, block_index, panel_map)
+    fits = (lists[2, 0] <= PASSED) & (lists[3, 0] <= LISTED)
+
+    def sparse(lists, table, activations, weight_tiles, panel_map, block_index, active_list, bias):
+        rows = activations.shape[0]
+        panels = lax.all_gather(weight_tiles[0], "rows", axis=0, tiled=True)
+        pool = exchange(lists, activations)
+        at = jnp.arange(rows, dtype=jnp.int32) // ROW_BLOCK
+        live = jnp.any(at[:, None] == active_list, axis=1, keepdims=True).astype(jnp.float32)
+        return sums(table, pool, panels, bias.reshape(PANELS, TILE), live)
+
+    def dense(lists, table, *rest):
+        return general(*rest)
+
+    return lax.cond(
+        fits, sparse, dense, lists, table, activations, weight_tiles, panel_map, block_index, active_list, bias
+    )
+
+
 def solution(mesh):
     in_specs = (
         P("rows", "cols"),

time: 586 us -> 291 us (0.50)
  waiting for transfers between devices: 293 us -> 0.7 us
  Pallas kernels: 0 us -> 263 us
  local copies, waits for them, and re-layouts: 149 us -> 7.99 us
  matrix products: 68 us -> 0 us
  other arithmetic: 61 us -> 0.76 us
    all_gather x2 -> x1, waiting for transfers between devices: 292 us -> 0.02 us  [sparse(): panels = lax.all_gather(weight_tiles[0], 'rows', axis=0, tiled=True)]
    pallas_call x0 -> x3, Pallas kernels: none -> 263 us  [the longest x1 215 us: exchange(): pl.pallas_call(exchange_kernel, out_shape=jax.ShapeDtypeStruct((SLOTS, ro...]
    gather x15 -> x0, local copies, waits for them, and re-layouts: 119 us -> none  [the longest x3 50.4 us: body(): jnp.take(gathered.reshape(blocks_here, ROW_BLOCK, -1), picked, axis=0)]
    dot_general x9 -> x0, matrix products: 68 us -> none  [the longest x8 63.3 us: body(): jnp.einsum('mpt,pts->mps', chosen, panel_block[:, depth], preferred_eleme...]
    select_n x9 -> x1, other arithmetic: 29.8 us -> 0.01 us  [sparse(): at = jnp.arange(rows, dtype=jnp.int32) // ROW_BLOCK]
    unnamed x1 -> x0, other arithmetic: 24 us -> none
    unnamed x31 -> x1, local copies, waits for them, and re-layouts: 24.4 us -> 0.82 us
  transfers between devices with their start and end apart: 2 -> 1, of which waited for: 1 -> 0; matrix products, arithmetic and copies ran while one was open for 30% -> 0% of each run, Pallas kernels for 0% -> 75%
where the time goes in v1:
time: 291 us; the launch traced here: 288 us
  Pallas kernels  263 us (90%)
  between operations  14.6 us (5%)
  local copies, waits for them, and re-layouts  7.99 us (3%)
    pallas_call x1, Pallas kernels, exchange(): pl.pallas_call(exchange_kernel, out_shape=jax.ShapeDtypeStruct((SLOTS, ro...  215 us
    pallas_call x1, Pallas kernels, sums(): pl.pallas_call(sums_kernel, out_shape=jax.ShapeDtypeStruct((rows, PANELS...  45.8 us
  transfers between devices with their start and end apart: 1, of which 0 were waited for; matrix products, arithmetic and copies ran while one was open for 0% of the time, Pallas kernels for 75%

profile of v1, /device:TPU:0, one launch (start us, length us, event | category | flops | bytes accessed | tf_op | source)
XLA Modules:
  0.0 287.7 jit_solution(14529395468621548406)
XLA Ops:
  6.5 0.8 copy.41.index_ref
  7.4 2.2 plan.1
  9.5 1.3 fusion.57
  12.0 268.8 %conditional.1 = (bf16[256,8192]{1,0:T(8,128)(2,1)}) conditional(s32[]{:T(128)} %bitcast.35, (s32[1,16]{1,0:T(1,128)}, s32[1,64]{1,0:T(1,128)}, bf16[256,16384]{1,0:T(8,128)(2,1)}, s32[256,8]{0,1:T(8,128)}, bf16[1,2,8,128,128]{4,3,2,1,0:T(8,128)(2,1)}, /*index=5*/f32[8192]{0:T(1024)}) %tuple.12, (s32[8,128]{1,0:T(8,128)}, ...), branch_computations={%region_0.3_spmd, %region_2.0_spmd} | conditional | flops 4487923712 | bytes 1007497600 | solution.py:302
  12.3 0.0 all-gather.10.cloned.1.call-start
  12.3 0.7 all-gather.10.cloned.1.call-update
  13.0 0.7 compare_reduce_fusion
  13.8 0.1 copy.36.refs_10_
  13.9 0.0 copy-start.10
  13.9 215.4 %exchange.1.refs_0_.refs_1_.refs_2_.refs_3_.refs_4_.refs_5_.refs_6_.refs_7_ = bf16[420,256,128]{2,1,0:T(8,128)(2,1)} custom-call(s32[8,128]{1,0:T(8,128)} %get-tuple-element.41.lists_ref, bf16[256,16384]{1,0:T(8,128)(2,1)} %get-tuple-element.42.act_ref), custom_call_target="tpu_custom_call" | custom-call | bytes 629145600 | tf_op jit(solution)/shard_map/cond/branch_1_fun/exchange/pallas_call | solution.py:194
  229.3 0.0 all-gather.10.cloned.1.call-done
  229.3 0.0 copy-done.10
  229.3 0.0 copy-start
  229.4 5.8 %copy-done = bf16[1,64,8,128,128]{4,3,2,0,1:T(8,128)(2,1)S(1)} copy-done((bf16[1,64,8,128,128]{4,3,2,0,1:T(8,128)(2,1)S(1)}, bf16[1,64,8,128,128]{4,3,2,0,1:T(8,128)(2,1)}, u32[]{:S(2)}) %copy-start) | copy-done | bytes 16777240 | tf_op jit(solution)/shard_map/cond
  235.1 45.8 %sums.1 = bf16[256,8192]{1,0:T(8,128)(2,1)} custom-call(s32[64,16]{1,0:T(8,128)S(1)} %get-tuple-element.40.table_ref, bf16[420,256,128]{2,1,0:T(8,128)(2,1)} %exchange.1.refs_0_.refs_1_.refs_2_.refs_3_.refs_4_.refs_5_.refs_6_.refs_7_, bf16[420,256,128]{2,1,0:T(8,128)(2,1)} %exchange.1.refs_0_.refs_1_.refs_2_.refs_3_.refs_4_.refs_5_.refs_6_.refs_7_, ...), custom_call_target="tpu_custom_call" | custom-call | flops 4294967296 | bytes 54525952 | tf_op jit(solution)/shard_map/cond/branch_1_fun/sums/pallas_call | solution.py:232
  (2 shorter events, 0.0 us)
Async XLA Ops:
  12.3 217.1 %all-gather.10.cloned.1.call-start = ((), (), s32[]{:S(2)}) async-start(), calls=%async_computation.2 | async-start | bytes 17301504 | tf_op jit(solution)/shard_map/cond/branch_1_fun/all_gather | solution.py:293
  13.9 215.4 %copy-start.10 = (f32[8192]{0:T(1024)S(1)}, f32[8192]{0:T(1024)}, u32[]{:S(2)}) copy-start(f32[8192]{0:T(1024)} %get-tuple-element.44) | copy-start | bytes 98308 | tf_op jit(solution)/shard_map/cond
  229.3 5.8 %copy-start = (bf16[1,64,8,128,128]{4,3,2,0,1:T(8,128)(2,1)S(1)}, bf16[1,64,8,128,128]{4,3,2,0,1:T(8,128)(2,1)}, u32[]{:S(2)}) copy-start(bf16[1,64,8,128,128]{4,3,2,0,1:T(8,128)(2,1)} %all-gather.10.cloned.1.call-done) | copy-start | bytes 50331652 | tf_op jit(solution)/shard_map/cond
Sparse Core Ops, SparseCore 0:
  15.4 75.0 all-gather.9

commit v2 on v1

--- a/solution.py
+++ b/solution.py
@@ -1,5 +1,3 @@
-import functools
-
 import jax
 import jax.numpy as jnp
 from jax import lax
@@ -20,6 +18,7 @@
 FAR_LEFT = RIGHT + LISTED
 FAR_RIGHT = FAR_LEFT + PASSED
 SLOTS = FAR_RIGHT + PASSED
+CHUNKS = (128, 96, 32)
 MESH = pl.DeviceIdType.MESH
 
 
@@ -134,119 +133,208 @@
     )(place, block_index, panel_map)
 
 
-def exchange_kernel(lists_ref, act_ref, pool_ref, act, to_right, to_left, send, recv, load, own):
+def neighbours():
     me = lax.axis_index("cols")
-    right, left = lax.rem(me + 1, GROUPS), lax.rem(me + GROUPS - 1, GROUPS)
-    reads = []
-    for s in range(HERE):
-        reads.append(pltpu.make_async_copy(act_ref.at[:, pl.ds(s * TILE, TILE)], act.at[s], load.at[s]))
-        reads[-1].start()
+    return lax.rem(me + 1, GROUPS), lax.rem(me + GROUPS - 1, GROUPS)
+
+
+def greet(right, left):
     barrier = pltpu.get_barrier_semaphore()
     for neighbour in (left, right):
         pl.semaphore_signal(barrier, inc=1, device_id={"cols": neighbour}, device_id_type=MESH)
-    for read in reads:
-        read.wait()
-
-    def pack(row, buffer, start, stop):
+    return barrier
+
+
+class Trade:
+    def __init__(self, lists_ref, act, pool, to_right, to_left, send, recv):
+        self.lists_ref, self.act, self.pool = lists_ref, act, pool
+        self.to_right, self.to_left, self.send, self.recv = to_right, to_left, send, recv
+        self.right, self.left = neighbours()
+
+    def pack(self, start, stop):
         def one(s, carry):
-            buffer[s] = act[lists_ref[row, s]]
+            self.to_right[s] = self.act[self.lists_ref[0, s]]
+            self.to_left[s] = self.act[self.lists_ref[1, s]]
             return carry
 
         lax.fori_loop(start, stop, one, 0)
 
-    def ship(n, src, dst, to):
+    def ship(self, n, src, dst, to):
         copy = pltpu.make_async_remote_copy(
             src_ref=src,
-            dst_ref=pool_ref.at[pl.ds(dst, src.shape[0])],
-            send_sem=send.at[n],
-            recv_sem=recv.at[n],
+            dst_ref=self.pool.at[pl.ds(dst, src.shape[0])],
+            send_sem=self.send.at[n],
+            recv_sem=self.recv.at[n],
             device_id={"cols": to},
             device_id_type=MESH,
         )
         copy.start()
         return copy
 
-    pack(0, to_right, 0, PASSED)
-    pack(1, to_left, 0, PASSED)
+    def heads(self):
+        self.head_right = self.ship(0, self.to_right.at[pl.ds(0, PASSED)], LEFT, self.right)
+        self.head_left = self.ship(1, self.to_left.at[pl.ds(0, PASSED)], RIGHT, self.left)
+
+    def tails(self):
+        rest = LISTED - PASSED
+        self.tail_right = self.ship(2, self.to_right.at[pl.ds(PASSED, rest)], LEFT + PASSED, self.right)
+        self.tail_left = self.ship(3, self.to_left.at[pl.ds(PASSED, rest)], RIGHT + PASSED, self.left)
+
+    def pass_on(self):
+        self.head_right.wait_recv()
+        self.on_right = self.ship(4, self.pool.at[pl.ds(LEFT, PASSED)], FAR_LEFT, self.right)
+        self.head_left.wait_recv()
+        self.on_left = self.ship(5, self.pool.at[pl.ds(RIGHT, PASSED)], FAR_RIGHT, self.left)
+
+    def finish(self):
+        self.head_right.wait_send()
+        self.head_left.wait_send()
+        for copy in (self.tail_right, self.tail_left, self.on_right, self.on_left):
+            copy.wait()
+
+
+def read_rows(act_ref, first, act, load):
+    reads = []
+    for s in range(HERE):
+        rows = pl.ds(first, act.shape[1])
+        reads.append(pltpu.make_async_copy(act_ref.at[rows, pl.ds(s * TILE, TILE)], act.at[s], load.at[s]))
+        reads[-1].start()
+    return reads
+
+
+def wait_all(copies):
+    for copy in copies:
+        copy.wait()
+
+
+def exchange_kernel(lists_ref, act_ref, pool_ref, act, to_right, to_left, send, recv, load, own):
+    trade = Trade(lists_ref, act, pool_ref, to_right, to_left, send, recv)
+    reads = read_rows(act_ref, 0, act, load)
+    barrier = greet(trade.right, trade.left)
+    wait_all(reads)
+    trade.pack(0, PASSED)
     pl.semaphore_wait(barrier, 2)
-    rest = LISTED - PASSED
-    head_right = ship(0, to_right.at[pl.ds(0, PASSED)], LEFT, right)
-    head_left = ship(1, to_left.at[pl.ds(0, PASSED)], RIGHT, left)
-    pack(0, to_right, PASSED, LISTED)
-    pack(1, to_left, PASSED, LISTED)
-    tail_right = ship(2, to_right.at[pl.ds(PASSED, rest)], LEFT + PASSED, right)
-    tail_left = ship(3, to_left.at[pl.ds(PASSED, rest)], RIGHT + PASSED, left)
+    trade.heads()
+    trade.pack(PASSED, LISTED)
+    trade.tails()
     keep = pltpu.make_async_copy(act, pool_ref.at[pl.ds(OWN, HERE)], own)
     keep.start()
-    head_right.wait_recv()
-    on_right = ship(4, pool_ref.at[pl.ds(LEFT, PASSED)], FAR_LEFT, right)
-    head_left.wait_recv()
-    on_left = ship(5, pool_ref.at[pl.ds(RIGHT, PASSED)], FAR_RIGHT, left)
-    head_right.wait_send()
-    head_left.wait_send()
+    trade.pass_on()
     keep.wait()
-    for copy in (tail_right, tail_left, on_right, on_left):
-        copy.wait()
+    trade.finish()
+
+
+def trade_scratch(rows):
+    return [
+        pltpu.VMEM((HERE, rows, TILE), jnp.bfloat16),
+        pltpu.VMEM((LISTED, rows, TILE), jnp.bfloat16),
+        pltpu.VMEM((LISTED, rows, TILE), jnp.bfloat16),
+        pltpu.SemaphoreType.DMA((6,)),
+        pltpu.SemaphoreType.DMA((6,)),
+        pltpu.SemaphoreType.DMA((HERE,)),
+        pltpu.SemaphoreType.DMA,
+    ]
 
 
 def exchange(lists, activations):
-    rows = activations.shape[0]
     return pl.pallas_call(
         exchange_kernel,
-        out_shape=jax.ShapeDtypeStruct((SLOTS, rows, TILE), jnp.bfloat16),
+        out_shape=jax.ShapeDtypeStruct((SLOTS, CHUNKS[0], TILE), jnp.bfloat16),
         in_specs=[pl.BlockSpec(memory_space=pltpu.SMEM), pl.BlockSpec(memory_space=pl.ANY)],
         out_specs=pl.BlockSpec(memory_space=pl.ANY),
-        scratch_shapes=[
-            pltpu.VMEM((HERE, rows, TILE), jnp.bfloat16),
-            pltpu.VMEM((LISTED, rows, TILE), jnp.bfloat16),
-            pltpu.VMEM((LISTED, rows, TILE), jnp.bfloat16),
-            pltpu.SemaphoreType.DMA((6,)),
-            pltpu.SemaphoreType.DMA((6,)),
-            pltpu.SemaphoreType.DMA((HERE,)),
-            pltpu.SemaphoreType.DMA,
-        ],
+        scratch_shapes=trade_scratch(CHUNKS[0]),
         compiler_params=pltpu.CompilerParams(
-            collective_id=0, has_side_effects=True, vmem_limit_bytes=40 << 20
+            collective_id=0, has_side_effects=True, vmem_limit_bytes=62 << 20
         ),
-        cost_estimate=pl.CostEstimate(flops=0, bytes_accessed=600 << 20, transcendentals=0),
+        cost_estimate=pl.CostEstimate(flops=0, bytes_accessed=300 << 20, transcendentals=0),
         name="exchange",
     )(lists, activations)
 
 
-def sums_kernel(table_ref, *refs):
-    taken, (weight_ref, bias_ref, live_ref, out_ref) = refs[:DEPTH], refs[DEPTH:]
-    j = pl.program_id(0)
-    inputs = jnp.concatenate([ref[0] for ref in taken], axis=1)
-    weights = weight_ref[0].reshape(DEPTH * TILE, TILE)
-    total = jnp.dot(inputs, weights, preferred_element_type=jnp.float32)
-    total = jnp.clip(total + bias_ref[pl.ds(j, 1), :], 0.0, 32.0)
-    out_ref[...] = jnp.where(live_ref[...] > 0.0, total, 0.0).astype(jnp.bfloat16)
-
-
-def sums(table, pool, panels, bias, live):
+def sums(table_ref, pool, weights, bias_ref, out_ref, first):
     rows = pool.shape[1]
-    taken = [
-        pl.BlockSpec((1, rows, TILE), functools.partial(lambda k, j, t: (t[j, k], 0, 0), k))
-        for k in range(DEPTH)
+    unroll = 4
+
+    def some(step, carry):
+        for u in range(unroll):
+            j = step * unroll + u
+            inputs = jnp.concatenate([pool[table_ref[j, k]] for k in range(DEPTH)], axis=1)
+            panel = weights[table_ref[j, DEPTH]].reshape(DEPTH * TILE, TILE)
+            total = jnp.dot(inputs, panel, preferred_element_type=jnp.float32)
+            total = jnp.clip(total + bias_ref[pl.ds(j, 1), :], 0.0, 32.0)
+            at = pl.ds(pl.multiple_of(j * TILE, TILE), TILE)
+            out_ref[pl.ds(first, rows), at] = total.astype(jnp.bfloat16)
+        return carry
+
+    lax.fori_loop(0, PANELS // unroll, some, 0)
+
+
+def layer_kernel(lists_ref, table_ref, act_ref, pool_ref, panels_ref, bias_ref, out_ref, *scratch):
+    per = 8
+    chunks = [scratch[n * per : (n + 1) * per] for n in range(len(CHUNKS) - 1)]
+    pool, weights, staged = scratch[-3:]
+    trades, reads, firsts = [], [], []
+    first = CHUNKS[0]
+    for n, (landed, act, to_right, to_left, send, recv, load, own) in enumerate(chunks):
+        trades.append(Trade(lists_ref, act, landed, to_right, to_left, send, recv))
+        reads.append(read_rows(act_ref, first, act, load))
+        firsts.append(first)
+        first += CHUNKS[n + 1]
+    barrier = greet(trades[0].right, trades[0].left)
+    stage = [
+        pltpu.make_async_copy(panels_ref, weights, staged.at[0]),
+        pltpu.make_async_copy(pool_ref, pool, staged.at[1]),
+    ]
+    for copy in stage:
+        copy.start()
+    keeps = []
+    for n, trade in enumerate(trades):
+        wait_all(reads[n])
+        trade.pack(0, PASSED)
+        if n == 0:
+            pl.semaphore_wait(barrier, 2)
+        trade.heads()
+        trade.pack(PASSED, LISTED)
+        if n == 0:
+            trade.tails()
+        keeps.append(pltpu.make_async_copy(trade.act, trade.pool.at[pl.ds(OWN, HERE)], chunks[n][-1]))
+        keeps[-1].start()
+    wait_all(stage)
+    sums(table_ref, pool, weights, bias_ref, out_ref, 0)
+    for n, trade in enumerate(trades):
+        trade.pass_on()
+        if n + 1 < len(trades):
+            trades[n + 1].tails()
+    for n, trade in enumerate(trades):
+        keeps[n].wait()
+        trade.finish()
+        sums(table_ref, trade.pool, weights, bias_ref, out_ref, firsts[n])
+
+
+def layer(lists, table, activations, pool, panels, bias):
+    rows = activations.shape[0]
+    scratch = []
+    for m in CHUNKS[1:]:
+        scratch += [pltpu.VMEM((SLOTS, m, TILE), jnp.bfloat16)] + trade_scratch(m)
+    scratch += [
+        pltpu.VMEM(pool.shape, jnp.bfloat16),
+        pltpu.VMEM(panels.shape, jnp.bfloat16),
+        pltpu.SemaphoreType.DMA((2,)),
     ]
     return pl.pallas_call(
-        sums_kernel,
+        layer_kernel,
         out_shape=jax.ShapeDtypeStruct((rows, PANELS * TILE), jnp.bfloat16),
-        grid_spec=pltpu.PrefetchScalarGridSpec(
-            num_scalar_prefetch=1,
-            grid=(PANELS,),
-            in_specs=taken
-            + [
-                pl.BlockSpec((1, DEPTH, TILE, TILE), lambda j, t: (t[j, DEPTH], 0, 0, 0)),
-                pl.BlockSpec((PANELS, TILE), lambda j, t: (0, 0)),
-                pl.BlockSpec((rows, 1), lambda j, t: (0, 0)),
-            ],
-            out_specs=pl.BlockSpec((rows, TILE), lambda j, t: (0, j)),
+        in_specs=[pl.BlockSpec(memory_space=pltpu.SMEM)] * 2
+        + [pl.BlockSpec(memory_space=pl.ANY)] * 3
+        + [pl.BlockSpec(memory_space=pltpu.VMEM)],
+        out_specs=pl.BlockSpec(memory_space=pltpu.VMEM),
+        scratch_shapes=scratch,
+        compiler_params=pltpu.CompilerParams(
+            collective_id=1, has_side_effects=True, vmem_limit_bytes=62 << 20
         ),
-        compiler_params=pltpu.CompilerParams(vmem_limit_bytes=32 << 20),
-        cost_estimate=pl.CostEstimate(flops=4 << 30, bytes_accessed=52 << 20, transcendentals=0),
-        name="sums",
-    )(table, *([pool] * DEPTH), panels, bias, live)
+        cost_estimate=pl.CostEstimate(flops=4 << 30, bytes_accessed=300 << 20, transcendentals=0),
+        name="layer",
+    )(lists, table, activations, pool, panels, bias)
 
 
 def general(activations, weight_tiles, panel_map, block_index, active_list, bias):
@@ -292,9 +380,10 @@
         rows = activations.shape[0]
         panels = lax.all_gather(weight_tiles[0], "rows", axis=0, tiled=True)
         pool = exchange(lists, activations)
+        out = layer(lists, table, activations, pool, panels, bias.reshape(PANELS, TILE))
         at = jnp.arange(rows, dtype=jnp.int32) // ROW_BLOCK
-        live = jnp.any(at[:, None] == active_list, axis=1, keepdims=True).astype(jnp.float32)
-        return sums(table, pool, panels, bias.reshape(PANELS, TILE), live)
+        live = jnp.any(at[:, None] == active_list, axis=1, keepdims=True)
+        return jnp.where(live, out, jnp.zeros_like(out))
 
     def dense(lists, table, *rest):
         return general(*rest)

time: 291 us -> 253 us (0.87)
  Pallas kernels: 263 us -> 230 us
  local copies, waits for them, and re-layouts: 7.99 us -> 4.1 us
    pallas_call x2, Pallas kernels: 261 us -> 228 us  [the longest x1 117 us: layer(): pl.pallas_call(layer_kernel, out_shape=jax.ShapeDtypeStruct((rows, PANELS...]
    cond x4 -> x6, local copies, waits for them, and re-layouts: 5.77 us -> 0.02 us
  transfers between devices with their start and end apart: 1 -> 1, of which waited for: 0 -> 0; matrix products, arithmetic and copies ran while one was open for 0% -> 0% of each run, Pallas kernels for 75% -> 44%
where the time goes in v2:
time: 253 us; the launch traced here: 252 us
  Pallas kernels  230 us (91%)
  between operations  14.6 us (6%)
  local copies, waits for them, and re-layouts  4.1 us (2%)
  other arithmetic  2.62 us (1%)
    pallas_call x1, Pallas kernels, layer(): pl.pallas_call(layer_kernel, out_shape=jax.ShapeDtypeStruct((rows, PANELS...  117 us
    pallas_call x1, Pallas kernels, exchange(): pl.pallas_call(exchange_kernel, out_shape=jax.ShapeDtypeStruct((SLOTS, CH...  111 us
  transfers between devices with their start and end apart: 1, of which 0 were waited for; matrix products, arithmetic and copies ran while one was open for 0% of the time, Pallas kernels for 44%

profile of v2, /device:TPU:0, one launch (start us, length us, event | category | flops | bytes accessed | tf_op | source)
XLA Modules:
  0.0 252.2 jit_solution(17564552264235920278)
XLA Ops:
  6.5 0.8 copy.37.index_ref
  7.4 2.2 plan.1
  9.5 1.3 fusion.57
  12.0 231.3 %conditional.1 = (bf16[256,8192]{1,0:T(8,128)(2,1)S(1)}) conditional(s32[]{:T(128)} %bitcast.34, (s32[1,16]{1,0:T(1,128)}, s32[1,64]{1,0:T(1,128)}, bf16[256,16384]{1,0:T(8,128)(2,1)}, s32[256,8]{0,1:T(8,128)}, bf16[1,2,8,128,128]{4,3,2,1,0:T(8,128)(2,1)}, /*index=5*/f32[8192]{0:T(1024)}) %tuple.12, (s32[1,16]{1,0:T(1,128)}, s32[8,128]{1,0:T(8,128)}, ...), branch_computations={%region_0.3_spmd, %region_2.0_spmd} | conditional | flops 4487923712 | bytes 1007497600 | solution.py:391
  12.3 0.0 all-gather.10.cloned.1.call-start
  12.3 0.7 all-gather.10.cloned.1.call-update
  13.0 0.0 copy-start.16
  13.0 0.0 copy-start.10
  13.0 0.0 copy-start.13
  13.0 110.9 %exchange.1.pool_ref = bf16[420,128,128]{2,1,0:T(8,128)(2,1)} custom-call(s32[8,128]{1,0:T(8,128)} %get-tuple-element.41.lists_ref, bf16[256,16384]{1,0:T(8,128)(2,1)} %get-tuple-element.43.act_ref), custom_call_target="tpu_custom_call" | custom-call | bytes 314572800 | tf_op jit(solution)/shard_map/cond/branch_1_fun/exchange/pallas_call | solution.py:240
  123.9 0.0 copy-done.16
  123.9 0.1 compare_reduce_fusion
  124.0 0.0 all-gather.10.cloned.1.call-done
  124.0 0.0 copy-done.10
  124.1 0.0 copy-done.13
  124.1 116.8 %layer.1 = bf16[256,8192]{1,0:T(8,128)(2,1)} custom-call(s32[8,128]{1,0:T(8,128)S(1)} %copy-done.13, s32[64,16]{1,0:T(8,128)S(1)} %get-tuple-element.42.table_ref, bf16[256,16384]{1,0:T(8,128)(2,1)} %get-tuple-element.43.act_ref, bf16[420,128,128]{2,1,0:T(8,128)(2,1)} %exchange.1.pool_ref, bf16[64,8,128,128]{3,2,1,0:T(8,128)(2,1)} %bitcast.86, ...), custom_call_target="tpu_custom_call" | custom-call | flops 4294967296 | bytes 314572800 | tf_op jit(solution)/shard_map/cond/branch_1_fun/layer/pallas_call | solution.py:324
  240.8 2.5 %broadcast_select_fusion = bf16[256,8192]{1,0:T(8,128)(2,1)S(1)} fusion(bf16[256,8192]{1,0:T(8,128)(2,1)} %layer.1, pred[256]{0:T(512)(128)(4,1)S(1)} %compare_reduce_fusion), kind=kLoop, calls=%fused_computation.12 | loop fusion | flops 2097152 | bytes 8388864 | tf_op jit(solution)/shard_map/cond/branch_1_fun/jit(_where)/select_n | solution.py:386
  243.4 0.0 copy-start.7
  243.4 2.0 copy-done.7
  (1 shorter events, 0.0 us)
Async XLA Ops:
  12.3 111.8 %all-gather.10.cloned.1.call-start = ((), (), s32[]{:S(2)}) async-start(), calls=%async_computation.2 | async-start | bytes 17301504 | tf_op jit(solution)/shard_map/cond/branch_1_fun/all_gather | solution.py:381
  13.0 110.9 %copy-start.16 = (s32[1,16]{1,0:T(1,128)S(1)}, s32[1,16]{1,0:T(1,128)}, u32[]{:S(2)}) copy-start(s32[1,16]{1,0:T(1,128)} %get-tuple-element.40) | copy-start | bytes 196 | tf_op jit(solution)/shard_map/cond
  13.0 111.0 %copy-start.10 = (f32[8192]{0:T(1024)S(1)}, f32[8192]{0:T(1024)}, u32[]{:S(2)}) copy-start(f32[8192]{0:T(1024)} %get-tuple-element.45) | copy-start | bytes 98308 | tf_op jit(solution)/shard_map/cond
  13.0 111.0 %copy-start.13 = (s32[8,128]{1,0:T(8,128)S(1)}, s32[8,128]{1,0:T(8,128)}, u32[]{:S(2)}) copy-start(s32[8,128]{1,0:T(8,128)} %get-tuple-element.41.lists_ref) | copy-start | bytes 12292 | tf_op jit(solution)/shard_map/cond
  243.4 2.0 copy-start.7
Sparse Core Ops, SparseCore 0:
  15.4 75.0 all-gather.9

commit v3 on v2

--- a/solution.py
+++ b/solution.py
@@ -1,3 +1,5 @@
+import functools
+
 import jax
 import jax.numpy as jnp
 from jax import lax
@@ -11,18 +13,25 @@
 PANELS = 64
 DEPTH = 8
 HERE = 128
-LISTED = 98
-PASSED = 48
+LIMITS = ((46, 94), (50, 100))
 OWN, LEFT = 0, HERE
-RIGHT = LEFT + LISTED
-FAR_LEFT = RIGHT + LISTED
-FAR_RIGHT = FAR_LEFT + PASSED
-SLOTS = FAR_RIGHT + PASSED
 CHUNKS = (128, 96, 32)
 MESH = pl.DeviceIdType.MESH
 
 
-def plan_kernel(place_ref, index_ref, map_ref, lists_ref, table_ref):
+class Sizes:
+    def __init__(self, passed, listed):
+        self.passed, self.listed = passed, listed
+        self.right = LEFT + listed
+        self.far_left = self.right + listed
+        self.far_right = self.far_left + passed
+        self.slots = self.far_right + passed
+
+
+SIZES = tuple(Sizes(*limits) for limits in LIMITS)
+
+
+def plan_kernel(place_ref, index_ref, map_ref, lists_ref, choice_ref, *table_refs):
     place = place_ref[0]
     blocks = GROUPS * HERE
     lane = lax.broadcasted_iota(jnp.int32, (GROUPS * PANELS, blocks), 1)
@@ -66,8 +75,13 @@
 
     at_right, passed_right, listed_right = order(by_right, right)
     at_left, passed_left, listed_left = order(by_left, left)
-    passed_most = jnp.max(jnp.maximum(passed_right, passed_left), axis=0, keepdims=True)
-    listed_most = jnp.max(jnp.maximum(listed_right, listed_left), axis=0, keepdims=True)
+    passed_most = jnp.max(jnp.maximum(passed_right, passed_left))
+    listed_most = jnp.max(jnp.maximum(listed_right, listed_left))
+    choice = jnp.int32(len(SIZES))
+    for n, size in reversed(list(enumerate(SIZES))):
+        fits = (passed_most <= size.passed) & (listed_most <= size.listed)
+        choice = jnp.where(fits, jnp.int32(n), choice)
+    choice_ref[0] = choice
 
     source = lax.broadcasted_iota(jnp.int32, (GROUPS, HERE), 0)
     mine = source == place
@@ -84,35 +98,29 @@
         [
             listing(at_right),
             listing(at_left),
-            jnp.broadcast_to(passed_most, (1, HERE)),
-            jnp.broadcast_to(listed_most, (1, HERE)),
-            jnp.zeros((4, HERE), jnp.float32),
+            jnp.zeros((6, HERE), jnp.float32),
         ],
         axis=0,
     ).astype(jnp.int32)
 
     ids_here = lax.broadcasted_iota(jnp.int32, (GROUPS, HERE), 1).astype(jnp.float32)
-    from_left = LEFT + at_right
-    from_right = RIGHT + at_left
-    from_far = jnp.where(by_right > 0.0, FAR_LEFT + at_right, FAR_RIGHT + at_left)
     away = lax.rem(source - place + GROUPS, GROUPS)
-    slots = jnp.where(
-        away == 0,
-        OWN + ids_here,
-        jnp.where(away == 1, from_right, jnp.where(away == 2, from_far, from_left)),
-    )
-    slots = jnp.concatenate([slots[s : s + 1] for s in range(GROUPS)], axis=1)
     mine_index = index_ref[pl.ds(pl.multiple_of(place * PANELS, PANELS), PANELS), :]
     lane = lax.broadcasted_iota(jnp.int32, (PANELS, blocks), 1)
-    columns = []
-    for k in range(DEPTH):
-        hit = mine_index[:, k : k + 1] == lane
-        columns.append(jnp.sum(jnp.where(hit, slots, 0.0), axis=1, keepdims=True))
     panel = lax.broadcasted_iota(jnp.int32, (PANELS, PANELS), 0)
     stored = lax.broadcasted_iota(jnp.int32, (PANELS, PANELS), 1).astype(jnp.float32)
-    columns.append(jnp.sum(jnp.where(map_ref[...] == panel, stored, 0.0), axis=1, keepdims=True))
-    columns.append(jnp.zeros((PANELS, 7), jnp.float32))
-    table_ref[...] = jnp.concatenate(columns, axis=1).astype(jnp.int32)
+    served = jnp.sum(jnp.where(map_ref[...] == panel, stored, 0.0), axis=1, keepdims=True)
+    for size, table_ref in zip(SIZES, table_refs):
+        from_far = jnp.where(by_right > 0.0, size.far_left + at_right, size.far_right + at_left)
+        near = jnp.where(away == 1, size.right + at_left, LEFT + at_right)
+        slots = jnp.where(away == 0, OWN + ids_here, jnp.where(away == 2, from_far, near))
+        slots = jnp.concatenate([slots[s : s + 1] for s in range(GROUPS)], axis=1)
+        columns = []
+        for k in range(DEPTH):
+            hit = mine_index[:, k : k + 1] == lane
+            columns.append(jnp.sum(jnp.where(hit, slots, 0.0), axis=1, keepdims=True))
+        columns += [served, jnp.zeros((PANELS, 7), jnp.float32)]
+        table_ref[...] = jnp.concatenate(columns, axis=1).astype(jnp.int32)
 
 
 def plan(place, block_index, panel_map):
@@ -120,14 +128,19 @@
         plan_kernel,
         out_shape=(
             jax.ShapeDtypeStruct((8, HERE), jnp.int32),
-            jax.ShapeDtypeStruct((PANELS, 16), jnp.int32),
-        ),
+            jax.ShapeDtypeStruct((1,), jnp.int32),
+        )
+        + (jax.ShapeDtypeStruct((PANELS, 16), jnp.int32),) * len(SIZES),
         in_specs=[
             pl.BlockSpec(memory_space=pltpu.SMEM),
             pl.BlockSpec(memory_space=pltpu.VMEM),
             pl.BlockSpec(memory_space=pltpu.VMEM),
         ],
-        out_specs=(pl.BlockSpec(memory_space=pltpu.VMEM), pl.BlockSpec(memory_space=pltpu.VMEM)),
+        out_specs=(
+            pl.BlockSpec(memory_space=pltpu.VMEM),
+            pl.BlockSpec(memory_space=pltpu.SMEM),
+        )
+        + (pl.BlockSpec(memory_space=pltpu.VMEM),) * len(SIZES),
         compiler_params=pltpu.CompilerParams(vmem_limit_bytes=16 << 20),
         name="plan",
     )(place, block_index, panel_map)
@@ -146,9 +159,10 @@
 
 
 class Trade:
-    def __init__(self, lists_ref, act, pool, to_right, to_left, send, recv):
+    def __init__(self, size, lists_ref, act, pool, to_right, to_left, send, recv):
         self.lists_ref, self.act, self.pool = lists_ref, act, pool
         self.to_right, self.to_left, self.send, self.recv = to_right, to_left, send, recv
+        self.size = size
         self.right, self.left = neighbours()
 
     def pack(self, start, stop):
@@ -172,19 +186,22 @@
         return copy
 
     def heads(self):
-        self.head_right = self.ship(0, self.to_right.at[pl.ds(0, PASSED)], LEFT, self.right)
-        self.head_left = self.ship(1, self.to_left.at[pl.ds(0, PASSED)], RIGHT, self.left)
+        first = pl.ds(0, self.size.passed)
+        self.head_right = self.ship(0, self.to_right.at[first], LEFT, self.right)
+        self.head_left = self.ship(1, self.to_left.at[first], self.size.right, self.left)
 
     def tails(self):
-        rest = LISTED - PASSED
-        self.tail_right = self.ship(2, self.to_right.at[pl.ds(PASSED, rest)], LEFT + PASSED, self.right)
-        self.tail_left = self.ship(3, self.to_left.at[pl.ds(PASSED, rest)], RIGHT + PASSED, self.left)
+        passed = self.size.passed
+        rest = pl.ds(passed, self.size.listed - passed)
+        self.tail_right = self.ship(2, self.to_right.at[rest], LEFT + passed, self.right)
+        self.tail_left = self.ship(3, self.to_left.at[rest], self.size.right + passed, self.left)
 
     def pass_on(self):
+        size = self.size
         self.head_right.wait_recv()
-        self.on_right = self.ship(4, self.pool.at[pl.ds(LEFT, PASSED)], FAR_LEFT, self.right)
+        self.on_right = self.ship(4, self.pool.at[pl.ds(LEFT, size.passed)], size.far_left, self.right)
         self.head_left.wait_recv()
-        self.on_left = self.ship(5, self.pool.at[pl.ds(RIGHT, PASSED)], FAR_RIGHT, self.left)
+        self.on_left = self.ship(5, self.pool.at[pl.ds(size.right, size.passed)], size.far_right, self.left)
 
     def finish(self):
         self.head_right.wait_send()
@@ -207,15 +224,15 @@
         copy.wait()
 
 
-def exchange_kernel(lists_ref, act_ref, pool_ref, act, to_right, to_left, send, recv, load, own):
-    trade = Trade(lists_ref, act, pool_ref, to_right, to_left, send, recv)
+def exchange_kernel(size, lists_ref, act_ref, pool_ref, act, to_right, to_left, send, recv, load, own):
+    trade = Trade(size, lists_ref, act, pool_ref, to_right, to_left, send, recv)
     reads = read_rows(act_ref, 0, act, load)
     barrier = greet(trade.right, trade.left)
     wait_all(reads)
-    trade.pack(0, PASSED)
+    trade.pack(0, size.passed)
     pl.semaphore_wait(barrier, 2)
     trade.heads()
-    trade.pack(PASSED, LISTED)
+    trade.pack(size.passed, size.listed)
     trade.tails()
     keep = pltpu.make_async_copy(act, pool_ref.at[pl.ds(OWN, HERE)], own)
     keep.start()
@@ -224,11 +241,11 @@
     trade.finish()
 
 
-def trade_scratch(rows):
+def trade_scratch(size, rows):
     return [
         pltpu.VMEM((HERE, rows, TILE), jnp.bfloat16),
-        pltpu.VMEM((LISTED, rows, TILE), jnp.bfloat16),
-        pltpu.VMEM((LISTED, rows, TILE), jnp.bfloat16),
+        pltpu.VMEM((size.listed, rows, TILE), jnp.bfloat16),
+        pltpu.VMEM((size.listed, rows, TILE), jnp.bfloat16),
         pltpu.SemaphoreType.DMA((6,)),
         pltpu.SemaphoreType.DMA((6,)),
         pltpu.SemaphoreType.DMA((HERE,)),
@@ -236,15 +253,16 @@
     ]
 
 
-def exchange(lists, activations):
+def exchange(n, lists, activations):
+    size = SIZES[n]
     return pl.pallas_call(
-        exchange_kernel,
-        out_shape=jax.ShapeDtypeStruct((SLOTS, CHUNKS[0], TILE), jnp.bfloat16),
+        functools.partial(exchange_kernel, size),
+        out_shape=jax.ShapeDtypeStruct((size.slots, CHUNKS[0], TILE), jnp.bfloat16),
         in_specs=[pl.BlockSpec(memory_space=pltpu.SMEM), pl.BlockSpec(memory_space=pl.ANY)],
         out_specs=pl.BlockSpec(memory_space=pl.ANY),
-        scratch_shapes=trade_scratch(CHUNKS[0]),
+        scratch_shapes=trade_scratch(size, CHUNKS[0]),
         compiler_params=pltpu.CompilerParams(
-            collective_id=0, has_side_effects=True, vmem_limit_bytes=62 << 20
+            collective_id=2 * n, has_side_effects=True, vmem_limit_bytes=62 << 20
         ),
         cost_estimate=pl.CostEstimate(flops=0, bytes_accessed=300 << 20, transcendentals=0),
         name="exchange",
@@ -269,14 +287,14 @@
     lax.fori_loop(0, PANELS // unroll, some, 0)
 
 
-def layer_kernel(lists_ref, table_ref, act_ref, pool_ref, panels_ref, bias_ref, out_ref, *scratch):
+def layer_kernel(size, lists_ref, table_ref, act_ref, pool_ref, panels_ref, bias_ref, out_ref, *scratch):
     per = 8
     chunks = [scratch[n * per : (n + 1) * per] for n in range(len(CHUNKS) - 1)]
     pool, weights, staged = scratch[-3:]
     trades, reads, firsts = [], [], []
     first = CHUNKS[0]
     for n, (landed, act, to_right, to_left, send, recv, load, own) in enumerate(chunks):
-        trades.append(Trade(lists_ref, act, landed, to_right, to_left, send, recv))
+        trades.append(Trade(size, lists_ref, act, landed, to_right, to_left, send, recv))
         reads.append(read_rows(act_ref, first, act, load))
         firsts.append(first)
         first += CHUNKS[n + 1]
@@ -290,11 +308,11 @@
     keeps = []
     for n, trade in enumerate(trades):
         wait_all(reads[n])
-        trade.pack(0, PASSED)
+        trade.pack(0, size.passed)
         if n == 0:
             pl.semaphore_wait(barrier, 2)
         trade.heads()
-        trade.pack(PASSED, LISTED)
+        trade.pack(size.passed, size.listed)
         if n == 0:
             trade.tails()
         keeps.append(pltpu.make_async_copy(trade.act, trade.pool.at[pl.ds(OWN, HERE)], chunks[n][-1]))
@@ -311,18 +329,18 @@
         sums(table_ref, trade.pool, weights, bias_ref, out_ref, firsts[n])
 
 
-def layer(lists, table, activations, pool, panels, bias):
-    rows = activations.shape[0]
+def layer(n, lists, table, activations, pool, panels, bias):
+    size, rows = SIZES[n], activations.shape[0]
     scratch = []
     for m in CHUNKS[1:]:
-        scratch += [pltpu.VMEM((SLOTS, m, TILE), jnp.bfloat16)] + trade_scratch(m)
+        scratch += [pltpu.VMEM((size.slots, m, TILE), jnp.bfloat16)] + trade_scratch(size, m)
     scratch += [
         pltpu.VMEM(pool.shape, jnp.bfloat16),
         pltpu.VMEM(panels.shape, jnp.bfloat16),
         pltpu.SemaphoreType.DMA((2,)),
     ]
     return pl.pallas_call(
-        layer_kernel,
+        functools.partial(layer_kernel, size),
         out_shape=jax.ShapeDtypeStruct((rows, PANELS * TILE), jnp.bfloat16),
         in_specs=[pl.BlockSpec(memory_space=pltpu.SMEM)] * 2
         + [pl.BlockSpec(memory_space=pl.ANY)] * 3
@@ -330,7 +348,7 @@
         out_specs=pl.BlockSpec(memory_space=pltpu.VMEM),
         scratch_shapes=scratch,
         compiler_params=pltpu.CompilerParams(
-            collective_id=1, has_side_effects=True, vmem_limit_bytes=62 << 20
+            collective_id=2 * n + 1, has_side_effects=True, vmem_limit_bytes=62 << 20
         ),
         cost_estimate=pl.CostEstimate(flops=4 << 30, bytes_accessed=300 << 20, transcendentals=0),
         name="layer",
@@ -372,25 +390,28 @@
 
 
 def body(activations, weight_tiles, panel_map, block_index, active_list, bias):
+    rows = activations.shape[0]
     place = lax.axis_index("cols").astype(jnp.int32).reshape(1)
-    lists, table = plan(place, block_index, panel_map)
-    fits = (lists[2, 0] <= PASSED) & (lists[3, 0] <= LISTED)
-
-    def sparse(lists, table, activations, weight_tiles, panel_map, block_index, active_list, bias):
-        rows = activations.shape[0]
-        panels = lax.all_gather(weight_tiles[0], "rows", axis=0, tiled=True)
-        pool = exchange(lists, activations)
-        out = layer(lists, table, activations, pool, panels, bias.reshape(PANELS, TILE))
-        at = jnp.arange(rows, dtype=jnp.int32) // ROW_BLOCK
-        live = jnp.any(at[:, None] == active_list, axis=1, keepdims=True)
-        return jnp.where(live, out, jnp.zeros_like(out))
-
-    def dense(lists, table, *rest):
+    lists, choice, *tables = plan(place, block_index, panel_map)
+
+    def sparse(n):
+        def branch(lists, tables, activations, weight_tiles, panel_map, block_index, active_list, bias):
+            panels = lax.all_gather(weight_tiles[0], "rows", axis=0, tiled=True)
+            pool = exchange(n, lists, activations)
+            return layer(n, lists, tables[n], activations, pool, panels, bias.reshape(PANELS, TILE))
+
+        return branch
+
+    def dense(lists, tables, *rest):
         return general(*rest)
 
-    return lax.cond(
-        fits, sparse, dense, lists, table, activations, weight_tiles, panel_map, block_index, active_list, bias
+    branches = [sparse(n) for n in range(len(SIZES))] + [dense]
+    out = lax.switch(
+        choice[0], branches, lists, tables, activations, weight_tiles, panel_map, block_index, active_list, bias
     )
+    at = jnp.arange(rows, dtype=jnp.int32) // ROW_BLOCK
+    live = jnp.any(at[:, None] == active_list, axis=1, keepdims=True)
+    return jnp.where(live, out, jnp.zeros_like(out))
 
 
 def solution(mesh):

time: 253 us -> 258 us (1.020)
  Pallas kernels: 230 us -> 236 us
  local copies, waits for them, and re-layouts: 4.1 us -> 0.83 us
  other arithmetic: 2.62 us -> 5.82 us
    pallas_call x2, Pallas kernels: 228 us -> 233 us  [the longest x1 120 us: layer(): pl.pallas_call(functools.partial(layer_kernel, size), out_shape=jax.Shape...]
where the time goes in v3:
time: 258 us; the launch traced here: 257 us
  Pallas kernels  236 us (91%)
  between operations  14 us (5%)
  other arithmetic  5.82 us (2%)
    pallas_call x1, Pallas kernels, layer(): pl.pallas_call(functools.partial(layer_kernel, size), out_shape=jax.Shape...  120 us
    pallas_call x1, Pallas kernels, exchange(): pl.pallas_call(functools.partial(exchange_kernel, size), out_shape=jax.Sh...  114 us
  transfers between devices with their start and end apart: 1, of which 0 were waited for; matrix products, arithmetic and copies ran while one was open for 0% of the time, Pallas kernels for 44%

profile of v3, /device:TPU:0, one launch (start us, length us, event | category | flops | bytes accessed | tf_op | source)
XLA Modules:
  0.0 257.3 jit_solution(6778688851599466284)
XLA Ops:
  6.5 1.3 compare_reduce_fusion
  7.8 0.8 copy.36.index_ref
  8.6 2.4 plan.1
  11.6 0.0 copy-start.15
  11.7 234.2 %conditional.1 = (bf16[256,8192]{1,0:T(8,128)(2,1)}) conditional(s32[]{:T(128)} %bitcast.37, (s32[8,128]{1,0:T(8,128)S(1)}, bf16[256,16384]{1,0:T(8,128)(2,1)}, bf16[1,2,8,128,128]{4,3,2,1,0:T(8,128)(2,1)}, f32[8192]{0:T(1024)}, s32[64,16]{1,0:T(8,128)S(1)}) %tuple.15, (s32[8,128]{1,0:T(8,128)S(1)}, bf16[256,16384]{1,0:T(8,128)(2,1)}, ...), branch_computations={%region_1.0_spmd, %region_2.3_spmd, %region_3.6_spmd} | conditional | flops 4487923712 | bytes 1007497600 | solution.py:409
  11.7 0.0 all-gather.10.cloned.1.call-start
  11.7 0.7 all-gather.10.cloned.1.call-update
  12.4 0.0 copy-start.9
  12.4 113.6 %exchange.3.pool_ref = bf16[428,128,128]{2,1,0:T(8,128)(2,1)} custom-call(s32[8,128]{1,0:T(8,128)S(1)} %get-tuple-element.47.lists_ref, bf16[256,16384]{1,0:T(8,128)(2,1)} %get-tuple-element.49.act_ref), custom_call_target="tpu_custom_call" | custom-call | bytes 314572800 | tf_op jit(solution)/shard_map/cond/branch_1_fun/exchange/pallas_call | solution.py:258
  126.0 0.0 all-gather.10.cloned.1.call-done
  126.0 0.0 copy-done.9
  126.0 119.6 %layer.3 = bf16[256,8192]{1,0:T(8,128)(2,1)} custom-call(s32[8,128]{1,0:T(8,128)S(1)} %get-tuple-element.47.lists_ref, s32[64,16]{1,0:T(8,128)S(1)} %get-tuple-element.48.table_ref, bf16[256,16384]{1,0:T(8,128)(2,1)} %get-tuple-element.49.act_ref, bf16[428,128,128]{2,1,0:T(8,128)(2,1)} %exchange.3.pool_ref, bf16[64,8,128,128]{3,2,1,0:T(8,128)(2,1)} %bitcast.90, ...), custom_call_target="tpu_custom_call" | custom-call | flops 4294967296 | bytes 314572800 | tf_op jit(solution)/shard_map/cond/branch_1_fun/layer/pallas_call | solution.py:342
  245.9 0.0 copy-done.15
  245.9 4.5 %broadcast_select_fusion.1 = bf16[256,8192]{1,0:T(8,128)(2,1)} fusion(bf16[256,8192]{1,0:T(8,128)(2,1)} %get-tuple-element.143, pred[256]{0:T(512)(128)(4,1)S(1)} %copy-done.15), kind=kLoop, calls=%fused_computation.124 | loop fusion | flops 2097152 | bytes 8388864 | tf_op jit(solution)/shard_map/jit(_where)/select_n | solution.py:414
  (1 shorter events, 0.0 us)
Async XLA Ops:
  11.6 234.2 %copy-start.15 = (pred[256]{0:T(512)(128)(4,1)S(1)}, pred[256]{0:T(512)(128)(4,1)}, u32[]{:S(2)}) copy-start(pred[256]{0:T(512)(128)(4,1)} %compare_reduce_fusion) | copy-start | bytes 772
  11.7 114.3 %all-gather.10.cloned.1.call-start = ((), (), s32[]{:S(2)}) async-start(), calls=%async_computation.1 | async-start | bytes 17301504 | tf_op jit(solution)/shard_map/cond/branch_1_fun/all_gather | solution.py:399
  12.4 113.6 %copy-start.9 = (f32[8192]{0:T(1024)S(1)}, f32[8192]{0:T(1024)}, u32[]{:S(2)}) copy-start(f32[8192]{0:T(1024)} %get-tuple-element.51) | copy-start | bytes 98308 | tf_op jit(solution)/shard_map/cond
Sparse Core Ops, SparseCore 0:
  14.8 75.0 all-gather.9

commit v4 on v3

--- a/solution.py
+++ b/solution.py
@@ -13,7 +13,7 @@
 PANELS = 64
 DEPTH = 8
 HERE = 128
-LIMITS = ((46, 94), (50, 100))
+LIMITS = ((44, 91), (45, 93), (47, 96), (50, 101))
 OWN, LEFT = 0, HERE
 CHUNKS = (128, 96, 32)
 MESH = pl.DeviceIdType.MESH
@@ -31,13 +31,15 @@
 SIZES = tuple(Sizes(*limits) for limits in LIMITS)
 
 
-def plan_kernel(place_ref, index_ref, map_ref, lists_ref, choice_ref, *table_refs):
+def plan_kernel(place_ref, index_ref, map_ref, lists_ref, choice_ref, *refs):
+    table_refs, index = refs[:-1], refs[-1]
     place = place_ref[0]
     blocks = GROUPS * HERE
+    index[...] = jnp.transpose(index_ref[...])
     lane = lax.broadcasted_iota(jnp.int32, (GROUPS * PANELS, blocks), 1)
     named = jnp.zeros((GROUPS * PANELS, blocks), jnp.float32)
     for k in range(DEPTH):
-        named = jnp.where(index_ref[:, k : k + 1] == lane, 1.0, named)
+        named = jnp.where(index[:, k : k + 1] == lane, 1.0, named)
     need = [jnp.max(named[c * PANELS : (c + 1) * PANELS], axis=0, keepdims=True) for c in range(GROUPS)]
 
     def asked(distance):
@@ -105,7 +107,7 @@
 
     ids_here = lax.broadcasted_iota(jnp.int32, (GROUPS, HERE), 1).astype(jnp.float32)
     away = lax.rem(source - place + GROUPS, GROUPS)
-    mine_index = index_ref[pl.ds(pl.multiple_of(place * PANELS, PANELS), PANELS), :]
+    mine_index = index[pl.ds(pl.multiple_of(place * PANELS, PANELS), PANELS), :]
     lane = lax.broadcasted_iota(jnp.int32, (PANELS, blocks), 1)
     panel = lax.broadcasted_iota(jnp.int32, (PANELS, PANELS), 0)
     stored = lax.broadcasted_iota(jnp.int32, (PANELS, PANELS), 1).astype(jnp.float32)
@@ -141,9 +143,10 @@
             pl.BlockSpec(memory_space=pltpu.SMEM),
         )
         + (pl.BlockSpec(memory_space=pltpu.VMEM),) * len(SIZES),
+        scratch_shapes=[pltpu.VMEM((GROUPS * PANELS, DEPTH), jnp.int32)],
         compiler_params=pltpu.CompilerParams(vmem_limit_bytes=16 << 20),
         name="plan",
-    )(place, block_index, panel_map)
+    )(place, block_index.T, panel_map)
 
 
 def neighbours():
@@ -158,20 +161,20 @@
     return barrier
 
 
+def pack(lists_ref, act, to_right, to_left, start, stop):
+    def one(s, carry):
+        to_right[s] = act[lists_ref[0, s]]
+        to_left[s] = act[lists_ref[1, s]]
+        return carry
+
+    lax.fori_loop(start, stop, one, 0)
+
+
 class Trade:
-    def __init__(self, size, lists_ref, act, pool, to_right, to_left, send, recv):
-        self.lists_ref, self.act, self.pool = lists_ref, act, pool
+    def __init__(self, size, pool, to_right, to_left, send, recv):
+        self.size, self.pool = size, pool
         self.to_right, self.to_left, self.send, self.recv = to_right, to_left, send, recv
-        self.size = size
         self.right, self.left = neighbours()
-
-    def pack(self, start, stop):
-        def one(s, carry):
-            self.to_right[s] = self.act[self.lists_ref[0, s]]
-            self.to_left[s] = self.act[self.lists_ref[1, s]]
-            return carry
-
-        lax.fori_loop(start, stop, one, 0)
 
     def ship(self, n, src, dst, to):
         copy = pltpu.make_async_remote_copy(
@@ -224,43 +227,57 @@
         copy.wait()
 
 
-def exchange_kernel(size, lists_ref, act_ref, pool_ref, act, to_right, to_left, send, recv, load, own):
-    trade = Trade(size, lists_ref, act, pool_ref, to_right, to_left, send, recv)
-    reads = read_rows(act_ref, 0, act, load)
+def exchange_kernel(size, lists_ref, act_ref, pool_ref, *refs):
+    later = len(CHUNKS) - 1
+    outs, scratch = refs[: 3 * later], refs[3 * later :]
+    packed = scratch[: 3 * (later + 1)]
+    send, recv, load, own = scratch[3 * (later + 1) :]
+    act, to_right, to_left = packed[:3]
+    trade = Trade(size, pool_ref, to_right, to_left, send, recv)
+    reads = read_rows(act_ref, 0, act, load.at[0])
     barrier = greet(trade.right, trade.left)
     wait_all(reads)
-    trade.pack(0, size.passed)
+    pack(lists_ref, act, to_right, to_left, 0, size.passed)
     pl.semaphore_wait(barrier, 2)
     trade.heads()
-    trade.pack(size.passed, size.listed)
+    pack(lists_ref, act, to_right, to_left, size.passed, size.listed)
     trade.tails()
-    keep = pltpu.make_async_copy(act, pool_ref.at[pl.ds(OWN, HERE)], own)
-    keep.start()
+    keeps = [pltpu.make_async_copy(act, pool_ref.at[pl.ds(OWN, HERE)], own.at[0])]
+    keeps[0].start()
+    first = CHUNKS[0]
+    for n in range(1, later + 1):
+        mine, right, left = packed[3 * n : 3 * n + 3]
+        wait_all(read_rows(act_ref, first, mine, load.at[n]))
+        pack(lists_ref, mine, right, left, 0, size.listed)
+        for k, ref in enumerate((mine, right, left)):
+            keeps.append(pltpu.make_async_copy(ref, outs[3 * (n - 1) + k], own.at[3 * n + k]))
+            keeps[-1].start()
+        first += CHUNKS[n]
     trade.pass_on()
-    keep.wait()
+    wait_all(keeps)
     trade.finish()
 
 
-def trade_scratch(size, rows):
-    return [
-        pltpu.VMEM((HERE, rows, TILE), jnp.bfloat16),
-        pltpu.VMEM((size.listed, rows, TILE), jnp.bfloat16),
-        pltpu.VMEM((size.listed, rows, TILE), jnp.bfloat16),
-        pltpu.SemaphoreType.DMA((6,)),
-        pltpu.SemaphoreType.DMA((6,)),
-        pltpu.SemaphoreType.DMA((HERE,)),
-        pltpu.SemaphoreType.DMA,
-    ]
+def packed_shapes(size, rows):
+    return [(HERE, rows, TILE), (size.listed, rows, TILE), (size.listed, rows, TILE)]
 
 
 def exchange(n, lists, activations):
     size = SIZES[n]
+    shapes = [packed_shapes(size, m) for m in CHUNKS]
+    out_shapes = [(size.slots, CHUNKS[0], TILE)] + sum(shapes[1:], [])
     return pl.pallas_call(
         functools.partial(exchange_kernel, size),
-        out_shape=jax.ShapeDtypeStruct((size.slots, CHUNKS[0], TILE), jnp.bfloat16),
+        out_shape=[jax.ShapeDtypeStruct(shape, jnp.bfloat16) for shape in out_shapes],
         in_specs=[pl.BlockSpec(memory_space=pltpu.SMEM), pl.BlockSpec(memory_space=pl.ANY)],
-        out_specs=pl.BlockSpec(memory_space=pl.ANY),
-        scratch_shapes=trade_scratch(size, CHUNKS[0]),
+        out_specs=[pl.BlockSpec(memory_space=pl.ANY)] * len(out_shapes),
+        scratch_shapes=[pltpu.VMEM(shape, jnp.bfloat16) for shape in sum(shapes, [])]
+        + [
+            pltpu.SemaphoreType.DMA((6,)),
+            pltpu.SemaphoreType.DMA((6,)),
+            pltpu.SemaphoreType.DMA((len(CHUNKS), HERE)),
+            pltpu.SemaphoreType.DMA((3 * len(CHUNKS),)),
+        ],
         compiler_params=pltpu.CompilerParams(
             collective_id=2 * n, has_side_effects=True, vmem_limit_bytes=62 << 20
         ),
@@ -269,9 +286,14 @@
     )(lists, activations)
 
 
-def sums(table_ref, pool, weights, bias_ref, out_ref, first):
+def sums(table_ref, active_ref, pool, weights, bias_ref, out_ref, first):
     rows = pool.shape[1]
     unroll = 4
+    at = lax.broadcasted_iota(jnp.int32, (rows, TILE), 0) // ROW_BLOCK + first // ROW_BLOCK
+    live = at == active_ref[0, 0]
+    for s in range(1, active_ref.shape[1]):
+        live = live | (at == active_ref[0, s])
+    most = jnp.where(live, 32.0, 0.0)
 
     def some(step, carry):
         for u in range(unroll):
@@ -279,7 +301,7 @@
             inputs = jnp.concatenate([pool[table_ref[j, k]] for k in range(DEPTH)], axis=1)
             panel = weights[table_ref[j, DEPTH]].reshape(DEPTH * TILE, TILE)
             total = jnp.dot(inputs, panel, preferred_element_type=jnp.float32)
-            total = jnp.clip(total + bias_ref[pl.ds(j, 1), :], 0.0, 32.0)
+            total = jnp.minimum(jnp.maximum(total + bias_ref[pl.ds(j, 1), :], 0.0), most)
             at = pl.ds(pl.multiple_of(j * TILE, TILE), TILE)
             out_ref[pl.ds(first, rows), at] = total.astype(jnp.bfloat16)
         return carry
@@ -287,15 +309,15 @@
     lax.fori_loop(0, PANELS // unroll, some, 0)
 
 
-def layer_kernel(size, lists_ref, table_ref, act_ref, pool_ref, panels_ref, bias_ref, out_ref, *scratch):
-    per = 8
-    chunks = [scratch[n * per : (n + 1) * per] for n in range(len(CHUNKS) - 1)]
-    pool, weights, staged = scratch[-3:]
-    trades, reads, firsts = [], [], []
+def layer_kernel(size, table_ref, active_ref, pool_ref, panels_ref, bias_ref, *refs):
+    later = len(CHUNKS) - 1
+    ins, out_ref, scratch = refs[: 3 * later], refs[3 * later], refs[3 * later + 1 :]
+    pools, (pool, weights, send, recv, staged) = scratch[:later], scratch[later:]
+    trades, firsts = [], []
     first = CHUNKS[0]
-    for n, (landed, act, to_right, to_left, send, recv, load, own) in enumerate(chunks):
-        trades.append(Trade(size, lists_ref, act, landed, to_right, to_left, send, recv))
-        reads.append(read_rows(act_ref, first, act, load))
+    for n in range(later):
+        mine, right, left = ins[3 * n : 3 * n + 3]
+        trades.append(Trade(size, pools[n], right, left, send.at[n], recv.at[n]))
         firsts.append(first)
         first += CHUNKS[n + 1]
     barrier = greet(trades[0].right, trades[0].left)
@@ -303,56 +325,53 @@
         pltpu.make_async_copy(panels_ref, weights, staged.at[0]),
         pltpu.make_async_copy(pool_ref, pool, staged.at[1]),
     ]
-    for copy in stage:
+    keeps = [
+        pltpu.make_async_copy(ins[3 * n], pools[n].at[pl.ds(OWN, HERE)], staged.at[2 + n]) for n in range(later)
+    ]
+    pl.semaphore_wait(barrier, 2)
+    trades[0].heads()
+    trades[0].tails()
+    for copy in stage + keeps:
         copy.start()
-    keeps = []
-    for n, trade in enumerate(trades):
-        wait_all(reads[n])
-        trade.pack(0, size.passed)
-        if n == 0:
-            pl.semaphore_wait(barrier, 2)
+    for trade in trades[1:]:
         trade.heads()
-        trade.pack(size.passed, size.listed)
-        if n == 0:
-            trade.tails()
-        keeps.append(pltpu.make_async_copy(trade.act, trade.pool.at[pl.ds(OWN, HERE)], chunks[n][-1]))
-        keeps[-1].start()
     wait_all(stage)
-    sums(table_ref, pool, weights, bias_ref, out_ref, 0)
+    sums(table_ref, active_ref, pool, weights, bias_ref, out_ref, 0)
     for n, trade in enumerate(trades):
         trade.pass_on()
-        if n + 1 < len(trades):
+        if n + 1 < later:
             trades[n + 1].tails()
     for n, trade in enumerate(trades):
         keeps[n].wait()
         trade.finish()
-        sums(table_ref, trade.pool, weights, bias_ref, out_ref, firsts[n])
-
-
-def layer(n, lists, table, activations, pool, panels, bias):
-    size, rows = SIZES[n], activations.shape[0]
-    scratch = []
-    for m in CHUNKS[1:]:
-        scratch += [pltpu.VMEM((size.slots, m, TILE), jnp.bfloat16)] + trade_scratch(size, m)
-    scratch += [
-        pltpu.VMEM(pool.shape, jnp.bfloat16),
-        pltpu.VMEM(panels.shape, jnp.bfloat16),
-        pltpu.SemaphoreType.DMA((2,)),
-    ]
+        sums(table_ref, active_ref, trade.pool, weights, bias_ref, out_ref, firsts[n])
+
+
+def layer(n, table, active_list, packed, panels, bias):
+    size, later = SIZES[n], len(CHUNKS) - 1
+    pool = packed[0]
     return pl.pallas_call(
         functools.partial(layer_kernel, size),
-        out_shape=jax.ShapeDtypeStruct((rows, PANELS * TILE), jnp.bfloat16),
+        out_shape=jax.ShapeDtypeStruct((sum(CHUNKS), PANELS * TILE), jnp.bfloat16),
         in_specs=[pl.BlockSpec(memory_space=pltpu.SMEM)] * 2
-        + [pl.BlockSpec(memory_space=pl.ANY)] * 3
-        + [pl.BlockSpec(memory_space=pltpu.VMEM)],
+        + [pl.BlockSpec(memory_space=pl.ANY)] * 2
+        + [pl.BlockSpec(memory_space=pltpu.VMEM)]
+        + [pl.BlockSpec(memory_space=pl.ANY)] * (3 * later),
         out_specs=pl.BlockSpec(memory_space=pltpu.VMEM),
-        scratch_shapes=scratch,
+        scratch_shapes=[pltpu.VMEM((size.slots, m, TILE), jnp.bfloat16) for m in CHUNKS[1:]]
+        + [
+            pltpu.VMEM(pool.shape, jnp.bfloat16),
+            pltpu.VMEM(panels.shape, jnp.bfloat16),
+            pltpu.SemaphoreType.DMA((later, 6)),
+            pltpu.SemaphoreType.DMA((later, 6)),
+            pltpu.SemaphoreType.DMA((2 + later,)),
+        ],
         compiler_params=pltpu.CompilerParams(
             collective_id=2 * n + 1, has_side_effects=True, vmem_limit_bytes=62 << 20
         ),
         cost_estimate=pl.CostEstimate(flops=4 << 30, bytes_accessed=300 << 20, transcendentals=0),
         name="layer",
-    )(lists, table, activations, pool, panels, bias)
+    )(table, active_list, pool, panels, bias, *packed[1:])
 
 
 def general(activations, weight_tiles, panel_map, block_index, active_list, bias):
@@ -390,15 +409,14 @@
 
 
 def body(activations, weight_tiles, panel_map, block_index, active_list, bias):
-    rows = activations.shape[0]
     place = lax.axis_index("cols").astype(jnp.int32).reshape(1)
     lists, choice, *tables = plan(place, block_index, panel_map)
 
     def sparse(n):
         def branch(lists, tables, activations, weight_tiles, panel_map, block_index, active_list, bias):
             panels = lax.all_gather(weight_tiles[0], "rows", axis=0, tiled=True)
-            pool = exchange(n, lists, activations)
-            return layer(n, lists, tables[n], activations, pool, panels, bias.reshape(PANELS, TILE))
+            packed = exchange(n, lists, activations)
+            return layer(n, tables[n], active_list, packed, panels, bias.reshape(PANELS, TILE))
 
         return branch
 
@@ -406,12 +424,9 @@
         return general(*rest)
 
     branches = [sparse(n) for n in range(len(SIZES))] + [dense]
-    out = lax.switch(
+    return lax.switch(
         choice[0], branches, lists, tables, activations, weight_tiles, panel_map, block_index, active_list, bias
     )
-    at = jnp.arange(rows, dtype=jnp.int32) // ROW_BLOCK
-    live = jnp.any(at[:, None] == active_list, axis=1, keepdims=True)
-    return jnp.where(live, out, jnp.zeros_like(out))
 
 
 def solution(mesh):

time: 258 us -> 235 us (0.911)
  Pallas kernels: 236 us -> 214 us
  other arithmetic: 5.82 us -> 0 us
  local copies, waits for them, and re-layouts: 0.83 us -> 4.65 us
    pallas_call x1, Pallas kernels: 120 us -> 106 us  [layer(): pl.pallas_call(functools.partial(layer_kernel, size), out_shape=jax.Shape...]
    pallas_call x1, Pallas kernels: 114 us -> 105 us  [exchange(): pl.pallas_call(functools.partial(exchange_kernel, size), out_shape=[jax.S...]
    select_n x2 -> x0, other arithmetic: 4.55 us -> none  [the longest x1 4.54 us: body(): return jnp.where(live, out, jnp.zeros_like(out))]
    unnamed x3 -> x1, local copies, waits for them, and re-layouts: 0.82 us -> 4.64 us
  transfers between devices with their start and end apart: 1 -> 1, of which waited for: 0 -> 0; matrix products, arithmetic and copies ran while one was open for 0% -> 0% of each run, Pallas kernels for 44% -> 45%
where the time goes in v4:
time: 235 us; the launch traced here: 234 us
  Pallas kernels  214 us (91%)
  between operations  14 us (6%)
  local copies, waits for them, and re-layouts  4.65 us (2%)
    pallas_call x1, Pallas kernels, layer(): pl.pallas_call(functools.partial(layer_kernel, size), out_shape=jax.Shape...  106 us
    pallas_call x1, Pallas kernels, exchange(): pl.pallas_call(functools.partial(exchange_kernel, size), out_shape=[jax.S...  105 us
  transfers between devices with their start and end apart: 1, of which 0 were waited for; matrix products, arithmetic and copies ran while one was open for 0% of the time, Pallas kernels for 45%

profile of v4, /device:TPU:0, one launch (start us, length us, event | category | flops | bytes accessed | tf_op | source)
XLA Modules:
  0.0 233.9 jit_solution(16214669931481468265)
XLA Ops:
  6.5 2.7 %plan.1 = (s32[8,128]{1,0:T(8,128)S(1)}, s32[1]{0:T(128)}, s32[64,16]{1,0:T(8,128)S(1)}, s32[64,16]{1,0:T(8,128)S(1)}, s32[64,16]{1,0:T(8,128)S(1)}, /*index=5*/s32[64,16]{1,0:T(8,128)S(1)}) custom-call(s32[1]{0:T(128)} %bitcast.41.place_ref, s32[8,256]{1,0:T(8,128)} %bitcast.116, s32[1,64]{1,0:T(1,128)} %map_ref.1), custom_call_target="tpu_custom_call" | custom-call | tf_op jit(solution)/shard_map/plan/pallas_call | solution.py:129
  9.8 212.6 %conditional.1 = (bf16[256,8192]{1,0:T(8,128)(2,1)}) conditional(s32[]{:T(128)} %bitcast.43, (s32[8,128]{1,0:T(8,128)S(1)}, bf16[256,16384]{1,0:T(8,128)(2,1)}, bf16[1,2,8,128,128]{4,3,2,1,0:T(8,128)(2,1)}, f32[8192]{0:T(1024)}, s32[64,16]{1,0:T(8,128)S(1)}, /*index=5*/s32[1,16]{1,0:T(1,128)}) %tuple.21, ...), branch_computations={%region_0.0_spmd, %region_1.0_spmd, %region_2.0_spmd, %region_3.0_... | conditional | flops 4487923712 | bytes 1007497600 | solution.py:427
  9.9 0.0 all-gather.12.cloned.1.call-start
  9.9 0.7 all-gather.12.cloned.1.call-update
  10.6 0.0 copy-start.8
  10.6 0.0 copy-start.15
  10.6 105.3 %exchange.4 = (bf16[398,128,128]{2,1,0:T(8,128)(2,1)}, bf16[128,96,128]{2,1,0:T(8,128)(2,1)}, bf16[91,96,128]{2,1,0:T(8,128)(2,1)}, bf16[91,96,128]{2,1,0:T(8,12...) custom-call(s32[8,128]{1,0:T(8,128)S(1)} %get-tuple-element.72.lists_ref, ...), custom_call_target="tpu_custom_call" | custom-call | bytes 314572800 | tf_op jit(solution)/shard_map/cond/branch_0_fun/exchange/pallas_call | solution.py:269
  116.0 0.0 all-gather.12.cloned.1.call-done
  116.0 0.0 copy-done.8
  116.0 0.0 copy-done.15
  116.0 106.2 %layer.4 = bf16[256,8192]{1,0:T(8,128)(2,1)} custom-call(s32[64,16]{1,0:T(8,128)S(1)} %get-tuple-element.62.table_ref, s32[1,16]{1,0:T(1,128)S(1)} %copy-done.15, bf16[398,128,128]{2,1,0:T(8,128)(2,1)} %get-tuple-element.76.pool_ref, bf16[64,8,128,128]{3,2,1,0:T(8,128)(2,1)} %bitcast.97, f32[64,128]{1,0:T(8,128)S(1)} %bitcast.112, ...), custom_call_target="tpu_custom_call" | custom-call | flops 4294967296 | bytes 314572800 | tf_op jit(solution)/shard_map/cond/branch_0_fun/layer/pallas_call | solution.py:353
  222.4 4.6 %copy.45 = bf16[256,8192]{1,0:T(8,128)(2,1)} copy(bf16[256,8192]{1,0:T(8,128)(2,1)} %get-tuple-element.143) | data formatting | bytes 8388608
Async XLA Ops:
  9.9 106.1 %all-gather.12.cloned.1.call-start = ((), (), s32[]{:S(2)}) async-start(), calls=%async_computation | async-start | bytes 17301504 | tf_op jit(solution)/shard_map/cond/branch_0_fun/all_gather | solution.py:417
  10.6 105.4 %copy-start.8 = (f32[8192]{0:T(1024)S(1)}, f32[8192]{0:T(1024)}, u32[]{:S(2)}) copy-start(f32[8192]{0:T(1024)} %get-tuple-element.78) | copy-start | bytes 98308 | tf_op jit(solution)/shard_map/cond
  10.6 105.4 %copy-start.15 = (s32[1,16]{1,0:T(1,128)S(1)}, s32[1,16]{1,0:T(1,128)}, u32[]{:S(2)}) copy-start(s32[1,16]{1,0:T(1,128)} %get-tuple-element.64.active_ref) | copy-start | bytes 196 | tf_op jit(solution)/shard_map/cond
Sparse Core Ops, SparseCore 0:
  13.0 75.0 all-gather.11

commit v5 on v4

v5 whole, which is shorter than its diff:
```python
import functools

import jax
import jax.numpy as jnp
from jax import lax
from jax.experimental import pallas as pl
from jax.experimental.pallas import tpu as pltpu
from jax.sharding import PartitionSpec as P

TILE = 128
ROW_BLOCK = 16
GROUPS = 4
PANELS = 64
DEPTH = 8
HERE = 128
LIMITS = ((46, 94), (50, 100))
OWN, LEFT = 0, HERE
BLOCKS = 16
UNIT = 8
RING = 4
FIRST = 8
SHARED = 14
SPARE = BLOCKS - SHARED
LATER = ((8, 1), (12, 2), (9, 3), (14, 2))
MIXED = 1
MESH = pl.DeviceIdType.MESH


class Sizes:
    def __init__(self, passed, listed):
        self.passed, self.listed = passed, listed
        self.right = LEFT + listed
        self.far_left = self.right + listed
        self.far_right = self.far_left + passed
        self.slots = self.far_right + passed


SIZES = tuple(Sizes(*limits) for limits in LIMITS)


def plan_kernel(place_ref, active_ref, index_ref, map_ref, weights_ref, lists_ref, choice_ref, *refs):
    table_refs, (held_ref, index, held, moved) = refs[:-4], refs[-4:]
    tiles = weights_ref.shape[0]
    bring = pltpu.make_async_copy(weights_ref, held.at[pl.ds(0, tiles)], moved.at[0])
    bring.start()
    column = lax.broadcasted_iota(jnp.int32, (ROW_BLOCK, TILE), 1)
    listed = jnp.zeros((ROW_BLOCK, TILE), jnp.int32)
    for s in range(BLOCKS):
        listed = jnp.where(column == s, active_ref[0, s], listed)
    held[pl.ds(tiles, ROW_BLOCK)] = listed.astype(jnp.float32).astype(jnp.bfloat16)
    bring.wait()
    leave = pltpu.make_async_copy(held, held_ref, moved.at[1])
    leave.start()
    place = place_ref[0]
    blocks = GROUPS * HERE
    index[...] = jnp.transpose(index_ref[...])
    lane = lax.broadcasted_iota(jnp.int32, (GROUPS * PANELS, blocks), 1)
    named = jnp.zeros((GROUPS * PANELS, blocks), jnp.float32)
    for k in range(DEPTH):
        named = jnp.where(index[:, k : k + 1] == lane, 1.0, named)
    need = [jnp.max(named[c * PANELS : (c + 1) * PANELS], axis=0, keepdims=True) for c in range(GROUPS)]

    def asked(distance):
        return jnp.concatenate(
            [need[(s + distance) % GROUPS][:, s * HERE : (s + 1) * HERE] for s in range(GROUPS)], axis=0
        )

    right, far, left = asked(1), asked(2), asked(3)
    row = lax.broadcasted_iota(jnp.int32, (HERE, HERE), 0)
    col = lax.broadcasted_iota(jnp.int32, (HERE, HERE), 1)
    before = (row < col).astype(jnp.bfloat16)

    def rank(flags):
        return jnp.dot(flags.astype(jnp.bfloat16), before, preferred_element_type=jnp.float32)

    def count(flags):
        return jnp.sum(flags, axis=1, keepdims=True)

    both = far * right * left
    none = far * (1.0 - right) * (1.0 - left)
    only_right = far * right * (1.0 - left)
    only_left = far * left * (1.0 - right)
    none_n, both_n = count(none), count(both)
    cut = jnp.clip(jnp.floor((count(left) - count(right) + none_n) * 0.5), 0.0, none_n)
    tilt = count(only_left) + none_n - cut - count(only_right) - cut
    share = jnp.clip(jnp.floor((tilt + both_n) * 0.5), 0.0, both_n)
    by_right = only_right + none * (rank(none) < cut) + both * (rank(both) < share)
    by_left = far - by_right

    def order(passed, wanted):
        rest = wanted * (1.0 - passed)
        at = jnp.where(passed > 0.0, rank(passed), count(passed) + rank(rest))
        inside = passed + rest
        return jnp.where(inside > 0.0, at, -1.0), count(passed), count(inside)

    at_right, passed_right, listed_right = order(by_right, right)
    at_left, passed_left, listed_left = order(by_left, left)
    passed_most = jnp.max(jnp.maximum(passed_right, passed_left))
    listed_most = jnp.max(jnp.maximum(listed_right, listed_left))
    choice = jnp.int32(len(SIZES))
    for n, size in reversed(list(enumerate(SIZES))):
        fits = (passed_most <= size.passed) & (listed_most <= size.listed)
        choice = jnp.where(fits, jnp.int32(n), choice)
    choice_ref[0] = choice

    source = lax.broadcasted_iota(jnp.int32, (GROUPS, HERE), 0)
    mine = source == place
    slot = lax.broadcasted_iota(jnp.int32, (HERE, HERE), 0).astype(jnp.float32)
    ids = lax.broadcasted_iota(jnp.int32, (8, HERE), 1).astype(jnp.bfloat16)

    def listing(at):
        own = jnp.sum(jnp.where(mine, at, 0.0), axis=0, keepdims=True)
        hot = (own == slot).astype(jnp.bfloat16)
        out = lax.dot_general(ids, hot, (((1,), (1,)), ((), ())), preferred_element_type=jnp.float32)
        return out[:1]

    lists_ref[...] = jnp.concatenate(
        [
            listing(at_right),
            listing(at_left),
            jnp.zeros((6, HERE), jnp.float32),
        ],
        axis=0,
    ).astype(jnp.int32)

    ids_here = lax.broadcasted_iota(jnp.int32, (GROUPS, HERE), 1).astype(jnp.float32)
    away = lax.rem(source - place + GROUPS, GROUPS)
    mine_index = index[pl.ds(pl.multiple_of(place * PANELS, PANELS), PANELS), :]
    lane = lax.broadcasted_iota(jnp.int32, (PANELS, blocks), 1)
    panel = lax.broadcasted_iota(jnp.int32, (PANELS, PANELS), 0)
    stored = lax.broadcasted_iota(jnp.int32, (PANELS, PANELS), 1).astype(jnp.float32)
    served = jnp.sum(jnp.where(map_ref[...] == panel, stored, 0.0), axis=1, keepdims=True)
    for size, table_ref in zip(SIZES, table_refs):
        from_far = jnp.where(by_right > 0.0, size.far_left + at_right, size.far_right + at_left)
        near = jnp.where(away == 1, size.right + at_left, LEFT + at_right)
        slots = jnp.where(away == 0, OWN + ids_here, jnp.where(away == 2, from_far, near))
        slots = jnp.concatenate([slots[s : s + 1] for s in range(GROUPS)], axis=1)
        columns = []
        for k in range(DEPTH):
            hit = mine_index[:, k : k + 1] == lane
            columns.append(jnp.sum(jnp.where(hit, slots, 0.0), axis=1, keepdims=True))
        holder = jnp.floor(served * 0.5)
        columns += [served - 2.0 * holder, holder, jnp.zeros((PANELS, 6), jnp.float32)]
        table_ref[...] = jnp.concatenate(columns, axis=1).astype(jnp.int32)
    leave.wait()


def plan(place, active_list, block_index, panel_map, tiles):
    held = (tiles.shape[0] + ROW_BLOCK, TILE)
    vmem, smem, anywhere = (pl.BlockSpec(memory_space=space) for space in (pltpu.VMEM, pltpu.SMEM, pl.ANY))
    return pl.pallas_call(
        plan_kernel,
        out_shape=(
            jax.ShapeDtypeStruct((8, HERE), jnp.int32),
            jax.ShapeDtypeStruct((1,), jnp.int32),
        )
        + (jax.ShapeDtypeStruct((PANELS, 16), jnp.int32),) * len(SIZES)
        + (jax.ShapeDtypeStruct(held, jnp.bfloat16),),
        in_specs=[smem, smem, vmem, vmem, anywhere],
        out_specs=(vmem, smem) + (vmem,) * len(SIZES) + (anywhere,),
        scratch_shapes=[
            pltpu.VMEM((GROUPS * PANELS, DEPTH), jnp.int32),
            pltpu.VMEM(held, jnp.bfloat16),
            pltpu.SemaphoreType.DMA((2,)),
        ],
        compiler_params=pltpu.CompilerParams(vmem_limit_bytes=16 << 20),
        name="plan",
    )(place, active_list, block_index.T, panel_map, tiles)


def neighbours():
    me = lax.axis_index("cols")
    return lax.rem(me + 1, GROUPS), lax.rem(me + GROUPS - 1, GROUPS)


class Place:
    def __init__(self):
        row = lax.axis_index("rows")
        self.unit = (row // UNIT) * UNIT
        self.at = row - self.unit
        self.ring, self.core = self.at // 2, lax.rem(self.at, 2)
        self.partner = self.unit + self.ring * 2 + 1 - self.core

    def along(self, distance):
        return lax.rem(self.ring + distance + RING, RING) * 2 + self.core

    def peers(self):
        return [self.unit + self.along(1), self.unit + self.along(-1), self.partner]


def greet(unit=None):
    barrier = pltpu.get_barrier_semaphore()
    others = [{"cols": neighbour} for neighbour in neighbours()]
    if unit is not None:
        others += [{"rows": peer} for peer in unit.peers()]
    for other in others:
        pl.semaphore_signal(barrier, inc=1, device_id=other, device_id_type=MESH)
    return barrier, len(others)


def remote(src, dst, send, recv, to):
    copy = pltpu.make_async_remote_copy(
        src_ref=src, dst_ref=dst, send_sem=send, recv_sem=recv, device_id=to, device_id_type=MESH
    )
    copy.start()
    return copy


def wait_all(copies):
    for copy in copies:
        copy.wait()


class Trade:
    def __init__(self, size, pool, to_right, to_left, send, recv):
        self.size, self.pool = size, pool
        self.to_right, self.to_left, self.send, self.recv = to_right, to_left, send, recv
        self.right, self.left = neighbours()

    def ship(self, n, src, dst, to):
        return remote(
            src, self.pool.at[pl.ds(dst, src.shape[0])], self.send.at[n], self.recv.at[n], {"cols": to}
        )

    def heads(self):
        first = pl.ds(0, self.size.passed)
        self.head_right = self.ship(0, self.to_right.at[first], LEFT, self.right)
        self.head_left = self.ship(1, self.to_left.at[first], self.size.right, self.left)

    def tails(self):
        passed = self.size.passed
        rest = pl.ds(passed, self.size.listed - passed)
        self.tail_right = self.ship(2, self.to_right.at[rest], LEFT + passed, self.right)
        self.tail_left = self.ship(3, self.to_left.at[rest], self.size.right + passed, self.left)

    def pass_on(self):
        size = self.size
        self.head_right.wait_recv()
        self.on_right = self.ship(4, self.pool.at[pl.ds(LEFT, size.passed)], size.far_left, self.right)
        self.head_left.wait_recv()
        self.on_left = self.ship(5, self.pool.at[pl.ds(size.right, size.passed)], size.far_right, self.left)

    def finish(self):
        self.head_right.wait_send()
        self.head_left.wait_send()
        wait_all((self.tail_right, self.tail_left, self.on_right, self.on_left))


class Spread:
    def __init__(self, unit, src, everyones, send, recv):
        self.unit, self.src, self.everyones, self.send, self.recv = unit, src, everyones, send, recv

    def start(self):
        self.copies = [self.ship(n, self.src, self.unit.at, peer) for n, peer in enumerate(self.unit.peers())]

    def ship(self, n, src, at, to):
        return remote(src, self.everyones.at[at], self.send.at[n], self.recv.at[n], {"rows": to})

    def again(self, n, distance, to):
        at = self.unit.along(distance)
        self.relayed.append(self.ship(n, self.everyones.at[at], at, to))

    def relay(self):
        self.relayed = []
        for copy in self.copies[:2]:
            copy.wait_recv()
        way = 1 - 2 * self.unit.core
        self.again(3, -way, self.unit.unit + self.unit.along(way))
        self.again(4, -1, self.unit.partner)
        self.again(5, 1, self.unit.partner)

    def relay_far(self):
        self.relayed[0].wait_recv()
        self.again(6, 2, self.unit.partner)

    def finish(self):
        for copy in self.copies[:2] + self.relayed[:1]:
            copy.wait_send()
        wait_all(self.copies[2:] + self.relayed[1:])


COPIES = 2 * RING - 1


def pack(lists_ref, slots, to_right, to_left, start, stop):
    def one(s, carry):
        to_right[s] = slots(lists_ref[0, s])
        to_left[s] = slots(lists_ref[1, s])
        return carry

    lax.fori_loop(start, stop, one, 0)


def compact(act, rows, to):
    def one(s, carry):
        for i, row in enumerate(rows):
            to[s, i] = act[s, row]
        return carry

    lax.fori_loop(0, to.shape[0], one, 0)


def exchange_kernel(size, lists_ref, active_ref, act_ref, pool_ref, spares_ref, *refs):
    groups = len(LATER)
    outs, scratch = refs[: 3 * groups], refs[3 * groups :]
    act, early, late, to_right, to_left = scratch[:5]
    packed = scratch[5 : 5 + 2 * groups]
    send, recv, spare_send, spare_recv, load, kept = scratch[5 + 2 * groups :]
    unit = Place()
    trade = Trade(size, pool_ref, to_right, to_left, send, recv)
    spread = Spread(unit, late.at[:, pl.ds(SHARED - FIRST, SPARE)], spares_ref, spare_send, spare_recv)

    def read(s):
        part = act_ref.at[:, :, pl.ds(pl.multiple_of(s * TILE, TILE), TILE)]
        return pltpu.make_async_copy(part, act.at[s], load.at[s])

    def begin(s, carry):
        read(s).start()
        return carry

    def end(s, carry):
        read(s).wait()
        return carry

    lax.fori_loop(0, HERE, begin, 0)
    barrier, met = greet(unit)
    rows = [jnp.minimum(active_ref[0, s], BLOCKS - 1) for s in range(BLOCKS)]
    lax.fori_loop(0, HERE, end, 0)
    compact(act, rows[:FIRST], early)
    pack(lists_ref, lambda block: early[block], to_right, to_left, 0, size.passed)
    pl.semaphore_wait(barrier, met)
    trade.heads()
    pack(lists_ref, lambda block: early[block], to_right, to_left, size.passed, size.listed)
    trade.tails()
    compact(act, rows[FIRST:], late)
    spread.start()
    keeps = [
        pltpu.make_async_copy(early, pool_ref.at[pl.ds(OWN, HERE)], kept.at[0]),
        pltpu.make_async_copy(spread.src, spares_ref.at[unit.at], kept.at[1]),
    ]
    for n, (first, slots) in enumerate(LATER):
        right, left = packed[2 * n : 2 * n + 2]
        part = pl.ds(first - FIRST, slots)
        pack(lists_ref, lambda block: late[block, part], right, left, 0, size.listed)
        for k, ref in enumerate((late.at[:, part], right, left)):
            keeps.append(pltpu.make_async_copy(ref, outs[3 * n + k], kept.at[2 + 3 * n + k]))
    for copy in keeps:
        copy.start()
    trade.pass_on()
    spread.relay()
    wait_all(keeps)
    spread.relay_far()
    trade.finish()
    spread.finish()


def packed_shapes(size, slots):
    return [(blocks, slots, ROW_BLOCK, TILE) for blocks in (HERE, size.listed, size.listed)]


def exchange(n, lists, active_list, activations):
    size = SIZES[n]
    width = activations.shape[1]
    later = [packed_shapes(size, slots) for _, slots in LATER]
    outs = [(size.slots, FIRST, ROW_BLOCK, TILE), (UNIT, HERE, SPARE, ROW_BLOCK, TILE)] + sum(later, [])
    scratch = [(HERE, slots, ROW_BLOCK, TILE) for slots in (BLOCKS, FIRST, BLOCKS - FIRST)]
    scratch += packed_shapes(size, FIRST)[1:] + sum([shapes[1:] for shapes in later], [])
    return pl.pallas_call(
        functools.partial(exchange_kernel, size),
        out_shape=[jax.ShapeDtypeStruct(shape, jnp.bfloat16) for shape in outs],
        in_specs=[pl.BlockSpec(memory_space=pltpu.SMEM)] * 2 + [pl.BlockSpec(memory_space=pl.ANY)],
        out_specs=[pl.BlockSpec(memory_space=pl.ANY)] * len(outs),
        scratch_shapes=[pltpu.VMEM(shape, jnp.bfloat16) for shape in scratch]
        + [
            pltpu.SemaphoreType.DMA((6,)),
            pltpu.SemaphoreType.DMA((6,)),
            pltpu.SemaphoreType.DMA((COPIES,)),
            pltpu.SemaphoreType.DMA((COPIES,)),
            pltpu.SemaphoreType.DMA((HERE,)),
            pltpu.SemaphoreType.DMA((2 + 3 * len(LATER),)),
        ],
        compiler_params=pltpu.CompilerParams(
            collective_id=3 * n, has_side_effects=True, vmem_limit_bytes=62 << 20
        ),
        cost_estimate=pl.CostEstimate(flops=0, bytes_accessed=300 << 20, transcendentals=0),
        name="exchange",
    )(lists, active_list, activations.reshape(BLOCKS, ROW_BLOCK, width))


def sums(table_ref, pool, weights, bias_ref, out_ref, slot):
    rows = pool.shape[1] * ROW_BLOCK
    unroll = 4

    def some(step, carry):
        for u in range(unroll):
            j = step * unroll + u
            taken = [pool[table_ref[j, k]].reshape(rows, TILE) for k in range(DEPTH)]
            panel = weights[table_ref[j, DEPTH], table_ref[j, DEPTH + 1]]
            total = jnp.dot(jnp.concatenate(taken, axis=1), panel, preferred_element_type=jnp.float32)
            total = jnp.clip(total + bias_ref[pl.ds(j, 1), :], 0.0, 32.0)
            at = pl.ds(pl.multiple_of(j * TILE, TILE), TILE)
            out_ref[pl.ds(slot * ROW_BLOCK, rows), at] = total.astype(jnp.bfloat16)
        return carry

    lax.fori_loop(0, PANELS // unroll, some, 0)


def levels(everyone_ref, unit):
    extra, room, extra_at, room_at = [], [], [jnp.int32(0)], [jnp.int32(0)]
    for v in range(UNIT):
        active = jnp.int32(0)
        for s in range(BLOCKS):
            active = active + jnp.where(everyone_ref[unit + v, s] < BLOCKS, 1, 0)
        extra.append(jnp.maximum(active - SHARED, 0))
        room.append(jnp.clip(SHARED - active, 0, SPARE))
        extra_at.append(extra_at[-1] + extra[-1])
        room_at.append(room_at[-1] + room[-1])
    return extra, room, extra_at, room_at


def hosted(everyone_ref, unit):
    extra, room, extra_at, room_at = levels(everyone_ref, unit.unit)
    mine, begin = jnp.int32(0), jnp.int32(0)
    for v in range(UNIT):
        mine = mine + jnp.where(unit.at == v, room[v], 0)
        begin = begin + jnp.where(unit.at == v, room_at[v], 0)
    guests = []
    for f in range(SPARE):
        turn = begin + f
        owner, which = jnp.int32(0), jnp.int32(0)
        for v in range(UNIT):
            hit = (turn >= extra_at[v]) & (turn < extra_at[v + 1])
            owner = owner + jnp.where(hit, v, 0)
            which = which + jnp.where(hit, turn - extra_at[v], 0)
        guests.append(((f < mine) & (turn < extra_at[UNIT]), owner, which))
    return guests


def layer_kernel(size, shared, lists_ref, everyone_ref, table_ref, pool_ref, spares_ref, panels_ref, bias_ref, *refs):
    groups = LATER[:-1] if shared else LATER
    count = len(groups)
    refs = list(refs)

    def take(n):
        part, refs[:n] = refs[:n], []
        return part

    ins, (out_ref,) = take(3 * count), take(1)
    returned_ref = take(1)[0] if shared else None
    pools, (pool, weights, send, recv, staged) = take(count), take(5)
    unit = Place() if shared else None
    lists = [ins[3 * n : 3 * n + 3] for n in range(count)]
    if shared:
        cast, mine, right, left, back_send, back_recv, cast_sem = refs
        given = lists[MIXED][0]
        lists[MIXED] = (mine, right, left)
        back = Spread(
            unit,
            out_ref.at[pl.ds(LATER[MIXED][0] * ROW_BLOCK, SPARE * ROW_BLOCK)],
            returned_ref,
            back_send,
            back_recv,
        )
    trades = [Trade(size, pools[n], lists[n][1], lists[n][2], send.at[n], recv.at[n]) for n in range(count)]
    barrier, met = greet(unit)
    loads = [
        pltpu.make_async_copy(panels_ref.at[:, pl.ds(n * DEPTH * TILE, DEPTH * TILE)], weights.at[n], staged.at[n])
        for n in range(weights.shape[0])
    ] + [pltpu.make_async_copy(pool_ref, pool, staged.at[2])]
    keeps = [
        pltpu.make_async_copy(lists[n][0], pools[n].at[pl.ds(OWN, HERE)], staged.at[3 + n]) for n in range(count)
    ]
    if shared:
        casting = [
            pltpu.make_async_copy(spares_ref, cast.at[pl.ds(0, UNIT)], cast_sem.at[0]),
            pltpu.make_async_copy(given, cast.at[UNIT], cast_sem.at[1]),
        ]
        for copy in casting:
            copy.start()
    pl.semaphore_wait(barrier, met)
    trades[0].heads()
    trades[0].tails()
    for n, copy in enumerate(keeps):
        if not (shared and n == MIXED):
            copy.start()
    if shared:
        guests = hosted(everyone_ref, unit)
        wait_all(casting)
        whose, which = [], []
        for i in range(SPARE):
            taken, owner, nth = guests[SPARE - 1 - i]
            whose.append(jnp.where(taken, owner, UNIT))
            which.append(jnp.where(taken, nth, i))

        def guest(s, carry):
            for i in range(SPARE):
                mine[s, i] = cast[whose[i], s, which[i]]
            return carry

        lax.fori_loop(0, HERE, guest, 0)
        pack(lists_ref, lambda block: mine[block], right, left, 0, size.listed)
        keeps[MIXED].start()
    trades[1].heads()
    trades[1].tails()
    for copy in loads:
        copy.start()
    trades[0].pass_on()
    wait_all(loads)
    sums(table_ref, pool, weights, bias_ref, out_ref, 0)
    trades[1].pass_on()
    for trade in trades[2:]:
        trade.heads()
        trade.tails()
    for n in [1, 0] + list(range(2, count)):
        trade = trades[n]
        keeps[n].wait()
        if n == 2:
            for other in trades[2:]:
                other.pass_on()
            if shared:
                back.relay()
        trade.finish()
        if shared and n == 2:
            back.relay_far()
        sums(table_ref, trade.pool, weights, bias_ref, out_ref, groups[n][0])
        if shared and n == MIXED:
            back.start()
    if shared:
        back.finish()


def layer(n, shared, lists, everyone, table, pool, spares, packed, panels, bias):
    size = SIZES[n]
    groups = LATER[:-1] if shared else LATER
    slots = SHARED if shared else BLOCKS
    width = PANELS * TILE
    outs = [jax.ShapeDtypeStruct((slots * ROW_BLOCK, width), jnp.bfloat16)]
    out_specs = [pl.BlockSpec(memory_space=pltpu.VMEM)]
    count = len(groups)
    scratch = [pltpu.VMEM((size.slots, m, ROW_BLOCK, TILE), jnp.bfloat16) for _, m in groups] + [
        pltpu.VMEM(pool.shape, jnp.bfloat16),
        pltpu.VMEM((2, panels.shape[0], DEPTH * TILE, TILE), jnp.bfloat16),
        pltpu.SemaphoreType.DMA((count, 6)),
        pltpu.SemaphoreType.DMA((count, 6)),
        pltpu.SemaphoreType.DMA((3 + count,)),
    ]
    if shared:
        outs.append(jax.ShapeDtypeStruct((UNIT, SPARE * ROW_BLOCK, width), jnp.bfloat16))
        out_specs.append(pl.BlockSpec(memory_space=pl.ANY))
        scratch += [pltpu.VMEM((UNIT + 1,) + spares.shape[1:], jnp.bfloat16)]
        scratch += [pltpu.VMEM(shape, jnp.bfloat16) for shape in packed_shapes(size, SPARE)]
        scratch += [
            pltpu.SemaphoreType.DMA((COPIES,)),
            pltpu.SemaphoreType.DMA((COPIES,)),
            pltpu.SemaphoreType.DMA((2,)),
        ]
    return pl.pallas_call(
        functools.partial(layer_kernel, size, shared),
        out_shape=outs,
        in_specs=[pl.BlockSpec(memory_space=pltpu.SMEM)] * 3
        + [pl.BlockSpec(memory_space=pl.ANY)] * 3
        + [pl.BlockSpec(memory_space=pltpu.VMEM)]
        + [pl.BlockSpec(memory_space=pl.ANY)] * (3 * count),
        out_specs=out_specs,
        scratch_shapes=scratch,
        compiler_params=pltpu.CompilerParams(
            collective_id=3 * n + (2 if shared else 1), has_side_effects=True, vmem_limit_bytes=62 << 20
        ),
        cost_estimate=pl.CostEstimate(flops=4 << 30, bytes_accessed=300 << 20, transcendentals=0),
        name="layer",
    )(lists, everyone, table, pool, spares, panels, bias, *packed[: 3 * count])


def place_kernel(shared, row_ref, everyone_ref, *refs):
    out_ref, returned_ref = refs[0], refs[1] if shared else None
    result_ref, stage, read, write = refs[-4:]
    row = row_ref[0]
    unit = (row // UNIT) * UNIT
    held = SHARED if shared else BLOCKS
    if shared:
        extra, room, extra_at, room_at = levels(everyone_ref, unit)
        begin = jnp.int32(0)
        for v in range(UNIT):
            begin = begin + jnp.where(row - unit == v, extra_at[v], 0)
    slots = []
    for b in range(BLOCKS):
        slot = jnp.int32(-1)
        for s in range(BLOCKS):
            slot = jnp.where(everyone_ref[row, s] == b, s, slot)
        slots.append(slot)

        @pl.when((slot >= 0) & (slot < held))
        def _():
            at = pl.multiple_of(slot * ROW_BLOCK, ROW_BLOCK)
            pltpu.make_async_copy(out_ref.at[pl.ds(at, ROW_BLOCK)], stage.at[b], read.at[b]).start()

        if shared:
            turn = begin + slot - SHARED
            host, nth = jnp.int32(0), jnp.int32(0)
            for v in range(UNIT):
                hit = (turn >= room_at[v]) & (turn < room_at[v + 1])
                host = host + jnp.where(hit, v, 0)
                nth = nth + jnp.where(hit, turn - room_at[v], 0)

            @pl.when(slot >= held)
            def _():
                at = pl.multiple_of((SPARE - 1 - nth) * ROW_BLOCK, ROW_BLOCK)
                pltpu.make_async_copy(returned_ref.at[host, pl.ds(at, ROW_BLOCK)], stage.at[b], read.at[b]).start()

    writes = []
    for b in range(BLOCKS):

        @pl.when(slots[b] < 0)
        def _():
            stage[b] = jnp.zeros(stage.shape[1:], stage.dtype)

        @pl.when(slots[b] >= 0)
        def _():
            pltpu.make_async_copy(out_ref.at[pl.ds(0, ROW_BLOCK)], stage.at[b], read.at[b]).wait()

        to = result_ref.at[pl.ds(b * ROW_BLOCK, ROW_BLOCK)]
        writes.append(pltpu.make_async_copy(stage.at[b], to, write.at[b]))
        writes[-1].start()
    wait_all(writes)


def place(shared, everyone, outs):
    row = lax.axis_index("rows").astype(jnp.int32).reshape(1)
    width = outs[0].shape[1]
    return pl.pallas_call(
        functools.partial(place_kernel, shared),
        out_shape=jax.ShapeDtypeStruct((BLOCKS * ROW_BLOCK, width), jnp.bfloat16),
        in_specs=[pl.BlockSpec(memory_space=pltpu.SMEM)] * 2 + [pl.BlockSpec(memory_space=pl.ANY)] * len(outs),
        out_specs=pl.BlockSpec(memory_space=pl.ANY),
        scratch_shapes=[
            pltpu.VMEM((BLOCKS, ROW_BLOCK, width), jnp.bfloat16),
            pltpu.SemaphoreType.DMA((BLOCKS,)),
            pltpu.SemaphoreType.DMA((BLOCKS,)),
        ],
        compiler_params=pltpu.CompilerParams(vmem_limit_bytes=62 << 20),
        name="place",
    )(row, everyone, *outs)


def general(activations, weight_tiles, panel_map, block_index, active_list, bias):
    row_count, local_width = activations.shape
    blocks_here = row_count // ROW_BLOCK
    listed = active_list[0]
    picked = jnp.minimum(listed, blocks_here - 1)
    gathered = lax.all_gather(activations, "cols", axis=1, tiled=True)
    compact = jnp.take(gathered.reshape(blocks_here, ROW_BLOCK, -1), picked, axis=0)
    slot_rows = compact.shape[0] * ROW_BLOCK
    tile_view = compact.reshape(slot_rows, -1, TILE)
    panels_here = panel_map.shape[1]
    columns = lax.axis_index("cols") * panels_here + panel_map[0]
    sources = jnp.take(block_index, columns, axis=0)
    panel_block = lax.all_gather(weight_tiles[0], "rows", axis=0, tiled=True)
    count_here = panel_block.shape[0]
    total = jnp.zeros((slot_rows, count_here, TILE), jnp.float32)
    for depth in range(panel_block.shape[1]):
        chosen = jnp.take(tile_view, sources[:, depth], axis=1)
        total = total + jnp.einsum(
            "mpt,pts->mps", chosen, panel_block[:, depth], preferred_element_type=jnp.float32
        )
    ordered = jnp.take(total, jnp.argsort(panel_map[0]), axis=1).reshape(slot_rows, -1)
    clamped = jnp.minimum(jnp.maximum(ordered + bias[None, :], 0.0), 32.0).astype(jnp.bfloat16)
    placing = (listed[:, None] == jnp.arange(blocks_here, dtype=jnp.int32)[None, :]).astype(
        jnp.bfloat16
    )
    spread = jnp.einsum(
        "sb,srw->brw",
        placing,
        clamped.reshape(listed.shape[0], ROW_BLOCK, -1),
        preferred_element_type=jnp.float32,
    )
    return spread.astype(jnp.bfloat16).reshape(row_count, -1)


def body(activations, weight_tiles, panel_map, block_index, active_list, bias):
    at = lax.axis_index("cols").astype(jnp.int32).reshape(1)
    lists, choice, *tables, held = plan(at, active_list, block_index, panel_map, weight_tiles.reshape(-1, TILE))

    def sparse(n):
        def branch(lists, tables, held, activations, weight_tiles, panel_map, block_index, active_list, bias):
            panels = lax.all_gather(held, "rows", axis=0, tiled=False)
            pool, spares, *packed = exchange(n, lists, active_list, activations)
            everyone = panels[:, held.shape[0] - ROW_BLOCK, :BLOCKS].astype(jnp.int32)
            active = jnp.sum(everyone < BLOCKS, axis=1, dtype=jnp.int32).reshape(-1, UNIT)
            left_over = jnp.maximum(active - SHARED, 0) - jnp.clip(SHARED - active, 0, SPARE)
            level = jnp.all(jnp.sum(left_over, axis=1) <= 0)
            biases = bias.reshape(PANELS, TILE)

            def finish(shared):
                def last(lists, everyone, table, pool, spares, packed, panels, biases):
                    outs = layer(n, shared, lists, everyone, table, pool, spares, packed, panels, biases)
                    return place(shared, everyone, outs)

                return last

            return lax.cond(
                level, finish(True), finish(False), lists, everyone, tables[n], pool, spares, packed, panels, biases
            )

        return branch

    def dense(lists, tables, held, *rest):
        return general(*rest)

    branches = [sparse(n) for n in range(len(SIZES))] + [dense]
    rest = (activations, weight_tiles, panel_map, block_index, active_list, bias)
    return lax.switch(choice[0], branches, lists, tables, held, *rest)


def solution(mesh):
    in_specs = (
        P("rows", "cols"),
        P("cols", "rows", None, None, None),
        P("cols", None),
        P(),
        P("rows", None),
        P("cols"),
    )
    out_specs = P("rows", "cols")
    return jax.shard_map(body, mesh=mesh, in_specs=in_specs, out_specs=out_specs, check_vma=False)
```

time: 235 us -> 224 us (0.953)
  Pallas kernels: 214 us -> 206 us
  local copies, waits for them, and re-layouts: 4.65 us -> 0.09 us
    pallas_call x1 -> x2, Pallas kernels: 106 us -> 91.4 us  [the longest x1 86.3 us: layer(): pl.pallas_call(functools.partial(layer_kernel, size, shared), out_shape=o...]
    pallas_call x1, Pallas kernels: 105 us -> 110 us  [exchange(): pl.pallas_call(functools.partial(exchange_kernel, size), out_shape=[jax.S...]
    unnamed x1 -> x0, local copies, waits for them, and re-layouts: 4.64 us -> none
  transfers between devices with their start and end apart: 1 -> 1, of which waited for: 0 -> 0; matrix products, arithmetic and copies ran while one was open for 0% -> 0% of each run, Pallas kernels for 45% -> 49%
where the time goes in v5:
time: 224 us
  Pallas kernels  206 us (92%)
  between operations  14 us (6%)
    pallas_call x1, Pallas kernels, exchange(): pl.pallas_call(functools.partial(exchange_kernel, size), out_shape=[jax.S...  110 us
    pallas_call x1, Pallas kernels, layer(): pl.pallas_call(functools.partial(layer_kernel, size, shared), out_shape=o...  86.3 us
    pallas_call x1, Pallas kernels, place(): pl.pallas_call(functools.partial(place_kernel, shared), out_shape=jax.Sha...  5.1 us
  transfers between devices with their start and end apart: 1, of which 0 were waited for; matrix products, arithmetic and copies ran while one was open for 0% of the time, Pallas kernels for 49%

profile of v5, /device:TPU:0, one launch (start us, length us, event | category | flops | bytes accessed | tf_op | source)
XLA Modules:
  0.0 223.5 jit_solution(12091064966769547103)
XLA Ops:
  6.5 4.2 %plan.1 = (s32[8,128]{1,0:T(8,128)S(1)}, s32[1]{0:T(128)}, s32[64,16]{1,0:T(8,128)}, s32[64,16]{1,0:T(8,128)}, bf16[2064,128]{1,0:T(8,128)(2,1)}) custom-call(s32[1]{0:T(128)} %bitcast.41.place_ref, s32[1,16]{1,0:T(1,128)} %active_ref.1, s32[8,256]{1,0:T(8,128)} %bitcast.124, s32[1,64]{1,0:T(1,128)} %map_ref.1, bf16[2048,128]{1,0:T(8,128)(2,1)} %bitcast.113), custom_call_target="tpu_custom_call" | custom-call | tf_op jit(solution)/shard_map/plan/pallas_call | solution.py:151
  11.3 205.3 %conditional.3 = (bf16[256,8192]{1,0:T(8,128)(2,1)}) conditional(s32[]{:T(128)} %bitcast.44, (bf16[2064,128]{1,0:T(8,128)(2,1)}, bf16[256,16384]{1,0:T(8,128)(2,1)}, s32[8,128]{1,0:T(8,128)S(1)}, s32[1,16]{1,0:T(1,128)}, f32[8192]{0:T(1024)}, /*index=5*/s32[64,16]{1,0:T(8,128)}) %tuple.27, (bf16[2064,128]{1,0:T(8,128)(2,1)}, ...), branch_computations={%region_0.6_spmd, %region_6.12_spmd, %region_12.15_spmd} | conditional | flops 4487923712 | bytes 1007497600 | solution.py:711
  11.3 0.0 all-gather.8.cloned.1.call-start
  11.4 0.7 all-gather.8.cloned.1.call-update
  12.1 0.0 copy-start.8
  12.1 110.4 %exchange.2 = (bf16[408,8,16,128]{3,2,1,0:T(8,128)(2,1)}, bf16[8,128,2,16,128]{4,3,2,1,0:T(8,128)(2,1)}, bf16[128,1,16,128]{3,2,1,0:T(8,128)(2,1)}, bf16[94,1,16...) custom-call(s32[8,128]{1,0:T(8,128)S(1)} %get-tuple-element.230.list, ...), custom_call_target="tpu_custom_call" | custom-call | bytes 314572800 | tf_op jit(solution)/shard_map/cond/branch_0_fun/exchange/pallas_call | solution.py:368
  122.5 0.0 all-gather.8.cloned.1.call-done
  122.5 0.9 slice_convert_fusion
  123.4 0.1 convert_reduce_fusion
  123.5 0.1 sub.21
  123.6 0.1 reduce_sum.33
  123.7 0.6 compare_reduce_fusion
  125.0 0.0 copy-done.8
  125.0 91.4 %conditional = (bf16[256,8192]{1,0:T(8,128)(2,1)}) conditional(s32[]{:T(128)} %convert_element_type.25, (s32[8,128]{1,0:T(8,128)S(1)}, s32[32,16]{1,0:T(8,128)S(1)}, s32[64,16]{1,0:T(8,128)}, bf16[408,8,16,128]{3,2,1,0:T(8,128)(2,1)}, bf16[8,128,2,16,128]{4,3,2,1,0:T(8,128)(2,1)}, /*index=5*/bf16[32,2064,128]{2,1,0:T(8,128)(2,1)}, ...), branch_computations={%region_4.4_spmd, %region_5.5_spmd} | conditional | flops 4294967296 | bytes 314572832 | solution.py:700
  125.0 86.3 %layer.5 = (bf16[224,8192]{1,0:T(8,128)(2,1)}, bf16[8,32,8192]{2,1,0:T(8,128)(2,1)}) custom-call(s32[8,128]{1,0:T(8,128)S(1)} %get-tuple-element.212.lists_ref, s32[32,16]{1,0:T(8,128)S(1)} %get-tuple-element.211.everyone_ref, s32[64,16]{1,0:T(8,128)} %get-tuple-element.213.table_ref, bf16[408,8,16,128]{3,2,1,0:T(8,128)(2,1)} %get-tuple-element.214.pool_ref, ...), custom_call_target="tpu_custom_call" | custom-call | flops 4294967296 | bytes 314572800 | tf_op jit(solution)/shard_map/cond/branch_0_fun/cond/branch_1_fun/layer/pallas_call | solution.py:557
  211.3 5.1 %place.5 = bf16[256,8192]{1,0:T(8,128)(2,1)} custom-call(s32[1]{0:T(128)} %bitcast.1.row_ref, s32[32,16]{1,0:T(8,128)S(1)} %get-tuple-element.211.everyone_ref, bf16[224,8192]{1,0:T(8,128)(2,1)} %get-tuple-element.227.refs_0_, bf16[8,32,8192]{2,1,0:T(8,128)(2,1)} %get-tuple-element.228.refs_1_), custom_call_target="tpu_custom_call" | custom-call | tf_op jit(solution)/shard_map/cond/branch_0_fun/cond/branch_1_fun/place/pallas_call | solution.py:630
  (1 shorter events, 0.0 us)
Async XLA Ops:
  11.3 111.2 %all-gather.8.cloned.1.call-start = ((), (), s32[]{:S(2)}) async-start(), calls=%async_computation | async-start | bytes 17436672 | tf_op jit(solution)/shard_map/cond/branch_0_fun/all_gather | solution.py:685
  12.1 112.9 %copy-start.8 = (f32[8192]{0:T(1024)S(1)}, f32[8192]{0:T(1024)}, u32[]{:S(2)}) copy-start(f32[8192]{0:T(1024)} %get-tuple-element.236) | copy-start | bytes 98308 | tf_op jit(solution)/shard_map/cond
Sparse Core Ops, SparseCore 0:
  14.5 92.0 all-gather.7

commit v6 on v5

--- a/solution.py
+++ b/solution.py
@@ -13,7 +13,7 @@
 PANELS = 64
 DEPTH = 8
 HERE = 128
-LIMITS = ((46, 94), (50, 100))
+LIMITS = ((45, 92), (47, 95), (50, 100))
 OWN, LEFT = 0, HERE
 BLOCKS = 16
 UNIT = 8
@@ -48,9 +48,6 @@
     for s in range(BLOCKS):
         listed = jnp.where(column == s, active_ref[0, s], listed)
     held[pl.ds(tiles, ROW_BLOCK)] = listed.astype(jnp.float32).astype(jnp.bfloat16)
-    bring.wait()
-    leave = pltpu.make_async_copy(held, held_ref, moved.at[1])
-    leave.start()
     place = place_ref[0]
     blocks = GROUPS * HERE
     index[...] = jnp.transpose(index_ref[...])
@@ -102,6 +99,9 @@
         fits = (passed_most <= size.passed) & (listed_most <= size.listed)
         choice = jnp.where(fits, jnp.int32(n), choice)
     choice_ref[0] = choice
+    bring.wait()
+    leave = pltpu.make_async_copy(held, held_ref, moved.at[1])
+    leave.start()
 
     source = lax.broadcasted_iota(jnp.int32, (GROUPS, HERE), 0)
     mine = source == place
@@ -326,10 +326,18 @@
     barrier, met = greet(unit)
     rows = [jnp.minimum(active_ref[0, s], BLOCKS - 1) for s in range(BLOCKS)]
     lax.fori_loop(0, HERE, end, 0)
-    compact(act, rows[:FIRST], early)
-    pack(lists_ref, lambda block: early[block], to_right, to_left, 0, size.passed)
+
+    def head(s, carry):
+        a, b = lists_ref[0, s], lists_ref[1, s]
+        for i in range(FIRST):
+            to_right[s, i] = act[a, rows[i]]
+            to_left[s, i] = act[b, rows[i]]
+        return carry
+
+    lax.fori_loop(0, size.passed, head, 0)
     pl.semaphore_wait(barrier, met)
     trade.heads()
+    compact(act, rows[:FIRST], early)
     pack(lists_ref, lambda block: early[block], to_right, to_left, size.passed, size.listed)
     trade.tails()
     compact(act, rows[FIRST:], late)
@@ -577,11 +585,6 @@
     row = row_ref[0]
     unit = (row // UNIT) * UNIT
     held = SHARED if shared else BLOCKS
-    if shared:
-        extra, room, extra_at, room_at = levels(everyone_ref, unit)
-        begin = jnp.int32(0)
-        for v in range(UNIT):
-            begin = begin + jnp.where(row - unit == v, extra_at[v], 0)
     slots = []
     for b in range(BLOCKS):
         slot = jnp.int32(-1)
@@ -594,16 +597,21 @@
             at = pl.multiple_of(slot * ROW_BLOCK, ROW_BLOCK)
             pltpu.make_async_copy(out_ref.at[pl.ds(at, ROW_BLOCK)], stage.at[b], read.at[b]).start()
 
-        if shared:
-            turn = begin + slot - SHARED
-            host, nth = jnp.int32(0), jnp.int32(0)
-            for v in range(UNIT):
-                hit = (turn >= room_at[v]) & (turn < room_at[v + 1])
-                host = host + jnp.where(hit, v, 0)
-                nth = nth + jnp.where(hit, turn - room_at[v], 0)
-
-            @pl.when(slot >= held)
+    if shared:
+        extra, room, extra_at, room_at = levels(everyone_ref, unit)
+        begin = jnp.int32(0)
+        for v in range(UNIT):
+            begin = begin + jnp.where(row - unit == v, extra_at[v], 0)
+        for b in range(BLOCKS):
+
+            @pl.when(slots[b] >= held)
             def _():
+                turn = begin + slots[b] - SHARED
+                host, nth = jnp.int32(0), jnp.int32(0)
+                for v in range(UNIT):
+                    hit = (turn >= room_at[v]) & (turn < room_at[v + 1])
+                    host = host + jnp.where(hit, v, 0)
+                    nth = nth + jnp.where(hit, turn - room_at[v], 0)
                 at = pl.multiple_of((SPARE - 1 - nth) * ROW_BLOCK, ROW_BLOCK)
                 pltpu.make_async_copy(returned_ref.at[host, pl.ds(at, ROW_BLOCK)], stage.at[b], read.at[b]).start()
 

time: 224 us -> 244 us (1.089)
  loops' own time: 0.98 us -> 19.2 us
    another operation x1, loops' own time: 0.95 us -> 18.8 us  [body(): return lax.switch(choice[0], branches, lists, tables, held, *rest)]
  transfers between devices with their start and end apart: 1 -> 1, of which waited for: 0 -> 0; matrix products, arithmetic and copies ran while one was open for 0% -> 0% of each run, Pallas kernels for 49% -> 46%
where the time goes in v6:
time: 244 us; the launch traced here: 242 us
  Pallas kernels  206 us (84%)
  loops' own time  19.2 us (8%)
  between operations  14.7 us (6%)
    pallas_call x1, Pallas kernels, exchange(): pl.pallas_call(functools.partial(exchange_kernel, size), out_shape=[jax.S...  111 us
    pallas_call x1, Pallas kernels, layer(): pl.pallas_call(functools.partial(layer_kernel, size, shared), out_shape=o...  87.4 us
    another operation x1, loops' own time, body(): return lax.switch(choice[0], branches, lists, tables, held, *rest)  18.8 us
  transfers between devices with their start and end apart: 1, of which 0 were waited for; matrix products, arithmetic and copies ran while one was open for 0% of the time, Pallas kernels for 46%

profile of v6, /device:TPU:0, one launch (start us, length us, event | category | flops | bytes accessed | tf_op | source)
XLA Modules:
  0.0 242.1 jit_solution(6431965163618783796)
XLA Ops:
  6.5 3.4 %plan.1 = (s32[8,128]{1,0:T(8,128)S(1)}, s32[1]{0:T(128)}, s32[64,16]{1,0:T(8,128)}, s32[64,16]{1,0:T(8,128)}, s32[64,16]{1,0:T(8,128)}, /*index=5*/bf16[2064,128]{1,0:T(8,128)(2,1)}) custom-call(s32[1]{0:T(128)} %bitcast.47.place_ref, s32[1,16]{1,0:T(1,128)} %active_ref.1, s32[8,256]{1,0:T(8,128)} %bitcast.139, s32[1,64]{1,0:T(1,128)} %map_ref.1, ...), custom_call_target="tpu_custom_call" | custom-call | tf_op jit(solution)/shard_map/plan/pallas_call | solution.py:151
  10.6 224.1 %conditional.4 = (bf16[256,8192]{1,0:T(8,128)(2,1)}) conditional(s32[]{:T(128)} %bitcast.50, (bf16[2064,128]{1,0:T(8,128)(2,1)}, bf16[256,16384]{1,0:T(8,128)(2,1)}, s32[8,128]{1,0:T(8,128)S(1)}, s32[1,16]{1,0:T(1,128)}, f32[8192]{0:T(1024)}, /*index=5*/s32[64,16]{1,0:T(8,128)}) %tuple.36, ...), branch_computations={%region_0.6_spmd, %region_6.12_spmd, %region_12.18_spmd, %region_1... | conditional | flops 4487923712 | bytes 1007497600 | solution.py:719
  10.6 0.0 all-gather.12.cloned.1.call-start
  10.7 0.7 all-gather.12.cloned.1.call-update
  11.3 0.0 copy-start.9
  11.4 110.7 %exchange.4 = (bf16[412,8,16,128]{3,2,1,0:T(8,128)(2,1)}, bf16[8,128,2,16,128]{4,3,2,1,0:T(8,128)(2,1)}, bf16[128,1,16,128]{3,2,1,0:T(8,128)(2,1)}, bf16[95,1,16...) custom-call(s32[8,128]{1,0:T(8,128)S(1)} %get-tuple-element.373.list, ...), custom_call_target="tpu_custom_call" | custom-call | bytes 314572800 | tf_op jit(solution)/shard_map/cond/branch_1_fun/exchange/pallas_call | solution.py:376
  122.1 0.0 all-gather.12.cloned.1.call-done
  122.1 0.9 slice_convert_fusion.1
  122.9 0.1 convert_reduce_fusion.1
  123.1 0.1 sub.34
  123.2 0.1 reduce_sum.51
  123.3 0.6 compare_reduce_fusion.1
  124.6 0.0 copy-done.9
  124.6 92.0 %conditional.1 = (bf16[256,8192]{1,0:T(8,128)(2,1)}) conditional(s32[]{:T(128)} %convert_element_type.37, (s32[8,128]{1,0:T(8,128)S(1)}, s32[32,16]{1,0:T(8,128)S(1)}, s32[64,16]{1,0:T(8,128)}, bf16[412,8,16,128]{3,2,1,0:T(8,128)(2,1)}, bf16[8,128,2,16,128]{4,3,2,1,0:T(8,128)(2,1)}, /*index=5*/bf16[32,2064,128]{2,1,0:T(8,128)(2,1)}, ...), branch_computations={%region_10.10_spmd, %region_11.11_spmd} | conditional | flops 4294967296 | bytes 314572832 | solution.py:708
  124.8 87.4 %layer.9 = (bf16[224,8192]{1,0:T(8,128)(2,1)}, bf16[8,32,8192]{2,1,0:T(8,128)(2,1)}) custom-call(s32[8,128]{1,0:T(8,128)S(1)} %get-tuple-element.355.lists_ref, s32[32,16]{1,0:T(8,128)S(1)} %get-tuple-element.354.everyone_ref, s32[64,16]{1,0:T(8,128)} %get-tuple-element.356.table_ref, bf16[412,8,16,128]{3,2,1,0:T(8,128)(2,1)} %get-tuple-element.357.pool_ref, ...), custom_call_target="tpu_custom_call" | custom-call | flops 4294967296 | bytes 314572800 | tf_op jit(solution)/shard_map/cond/branch_1_fun/cond/branch_1_fun/layer/pallas_call | solution.py:565
  212.1 4.3 %place.9 = bf16[256,8192]{1,0:T(8,128)(2,1)} custom-call(s32[1]{0:T(128)} %bitcast.7.row_ref, s32[32,16]{1,0:T(8,128)S(1)} %get-tuple-element.354.everyone_ref, bf16[224,8192]{1,0:T(8,128)(2,1)} %get-tuple-element.370.refs_0_, bf16[8,32,8192]{2,1,0:T(8,128)(2,1)} %get-tuple-element.371.refs_1_), custom_call_target="tpu_custom_call" | custom-call | tf_op jit(solution)/shard_map/cond/branch_1_fun/cond/branch_1_fun/place/pallas_call | solution.py:638
  (1 shorter events, 0.0 us)
Async XLA Ops:
  10.6 111.5 %all-gather.12.cloned.1.call-start = ((), (), s32[]{:S(2)}) async-start(), calls=%async_computation.1 | async-start | bytes 17436672 | tf_op jit(solution)/shard_map/cond/branch_1_fun/all_gather | solution.py:693
  11.3 113.2 %copy-start.9 = (f32[8192]{0:T(1024)S(1)}, f32[8192]{0:T(1024)}, u32[]{:S(2)}) copy-start(f32[8192]{0:T(1024)} %get-tuple-element.379) | copy-start | bytes 98308 | tf_op jit(solution)/shard_map/cond
Sparse Core Ops, SparseCore 0:
  13.8 92.0 all-gather.11
